TPU v7x, 128 devices: a whole 4x4x4 slice. The times are simulated.
128 devices in a mesh: dp: 16 (over z, y), value: 8 (over x, core).
Axes of the slice: x: 4, y: 4, z: 4, core: 2. Of those that a mesh axis runs over, the one named last changes fastest.
Arguments:
- inputs: bfloat16 [4, 512, 2048], P(None, 'dp'), may hold values from -6 to 6
- qk_weight: bfloat16 [2048, 4096], P(None, 'value'), may hold values from -0.125 to 0.125
- value_weight: bfloat16 [2048, 4096], P(None, 'value'), may hold values from -0.125 to 0.125
- output_gate_weight: bfloat16 [2048, 4096], P(None, 'value'), may hold values from -0.125 to 0.125
- rate_weight: bfloat16 [2048, 64], replicated, may hold values from -0.125 to 0.125
- log_decay: float32 [32], replicated, may hold values from -2.5 to 1.5
- decay_bias: float32 [32], replicated, may hold values from -1 to 1
- norm_gain: float32 [128], P('value'), may hold values from 0.1 to 1.9
- out_weight: bfloat16 [4096, 2048], P('value'), may hold values from -0.09375 to 0.09375
- states: float32 [512, 128, 32, 128], P('dp', 'value'), may hold values from -60 to 60, as said below
- prefilled: float32 [256, 128, 32, 128], P('dp', 'value'), may hold values from -60 to 60, as said below
- finished: int32 [4, 16, 2], replicated, may hold values from 0 to 31, as said below
- new_owner: int32 [4, 16, 2], replicated, may hold values from 0 to 15, as said below
- new_slot: int32 [4, 16, 2], replicated, may hold values from 0 to 15, as said below
Outputs:
- hidden_out: bfloat16 [4, 512, 2048], P(None, 'dp', 'value')
Inputs may be any that keep to these rules, and one draw needn't show every extreme that they name: `states`: entries of a row are independent; the value entries have different scales. `prefilled`: drawn like states. `finished`: the 2 rows of one dp index in one step are distinct. `new_owner`: over all 4 steps, no two replacing rows of one dp index have the same owner. `new_slot`: no prefilled state is used twice.
All inputs are finite; a program needn't handle non-finite values.
Results may differ from a plain program's by a relative error of at most 0.006.
Values may be sent and summed in bfloat16 or wider, within the bound.
A program may use at most 128 MiB of HBM per device.

v0:
```python
import jax
import jax.numpy as jnp
from jax import lax
from jax.sharding import PartitionSpec as P

KH = 16
DK = 128
DV = 128


def normalized(heads):
    return heads * lax.rsqrt(jnp.sum(heads * heads, axis=-1, keepdims=True) + 1e-06)


def outgoing_states(owners, slots, owner_id, prefilled):
    served = owners == owner_id
    chosen = jnp.sum(jnp.where(served, slots, 0), axis=1)
    available_mask = jnp.any(served, axis=1)
    picked = jnp.take(prefilled, chosen, axis=0)
    return jnp.where(available_mask[:, None, None, None], picked, 0.0)


def advance(
    states,
    inputs_now,
    qk_weight,
    value_weight,
    output_gate_weight,
    rate_weight,
    log_decay,
    decay_bias,
    norm_gain,
    out_weight,
):
    row_count = inputs_now.shape[0]
    head_count = log_decay.shape[0]
    local_entries = norm_gain.shape[0]
    joined = jnp.dot(inputs_now, qk_weight, preferred_element_type=jnp.float32).astype(jnp.bfloat16)
    joined = lax.all_gather(joined, "value", axis=1, tiled=True).astype(jnp.float32)
    split_at = KH * DK
    repeats = head_count // KH
    queries = normalized(joined[:, :split_at].reshape(row_count, KH, DK)) * DK ** (-0.5)
    keys = normalized(joined[:, split_at:].reshape(row_count, KH, DK))
    queries = jnp.repeat(queries, repeats, axis=1)
    keys = jnp.repeat(keys, repeats, axis=1)
    values = jnp.dot(inputs_now, value_weight, preferred_element_type=jnp.float32).reshape(
        row_count, local_entries, head_count
    )
    gating = jnp.dot(inputs_now, output_gate_weight, preferred_element_type=jnp.float32).reshape(
        row_count, local_entries, head_count
    )
    rates = jnp.dot(inputs_now, rate_weight, preferred_element_type=jnp.float32)
    strength = jax.nn.sigmoid(rates[:, :head_count])
    retain = jnp.exp(-jnp.exp(log_decay) * jax.nn.softplus(rates[:, head_count:] + decay_bias))
    decayed = states * retain[:, None, :, None]
    memory = jnp.sum(decayed * keys[:, None], axis=-1)
    update = (values - memory) * strength[:, None, :]
    states = decayed + update[..., None] * keys[:, None]
    readout = jnp.sum(states * queries[:, None], axis=-1)
    squares = lax.psum(jnp.sum(readout * readout, axis=1), "value")
    scaling = lax.rsqrt(squares / DV + 1e-06)
    gated = readout * scaling[:, None, :] * norm_gain[None, :, None] * jax.nn.silu(gating)
    gated = gated.astype(jnp.bfloat16).reshape(row_count, local_entries * head_count)
    columns = lax.psum_scatter(
        lax.dot_general(
            out_weight, gated, (((0,), (1,)), ((), ())), preferred_element_type=jnp.float32
        ),
        "value",
        scatter_dimension=0,
        tiled=True,
    )
    return (states, columns.T.astype(jnp.bfloat16))


def on_device(
    inputs,
    qk_weight,
    value_weight,
    output_gate_weight,
    rate_weight,
    log_decay,
    decay_bias,
    norm_gain,
    out_weight,
    states,
    prefilled,
    finished,
    new_owner,
    new_slot,
):
    owner_id = lax.axis_index("dp")
    step_count = inputs.shape[0]
    replaced = finished.shape[2]
    results = []
    for moment in range(step_count):
        my_rows = lax.dynamic_index_in_dim(finished[moment], owner_id, 0, False)
        my_owners = lax.dynamic_index_in_dim(new_owner[moment], owner_id, 0, False)
        outgoing = outgoing_states(new_owner[moment], new_slot[moment], owner_id, prefilled)
        arrived = lax.all_to_all(outgoing, "dp", split_axis=0, concat_axis=0, tiled=True)
        for member in range(replaced):
            fresh = lax.dynamic_index_in_dim(arrived, my_owners[member], 0, False)
            states = lax.dynamic_update_index_in_dim(states, fresh, my_rows[member], 0)
        states, produced = advance(
            states,
            inputs[moment],
            qk_weight,
            value_weight,
            output_gate_weight,
            rate_weight,
            log_decay,
            decay_bias,
            norm_gain,
            out_weight,
        )
        results.append(produced)
    return jnp.stack(results)


def solution(mesh):
    return jax.shard_map(
        on_device,
        mesh=mesh,
        in_specs=(
            P(None, "dp", None),
            P(None, "value"),
            P(None, "value"),
            P(None, "value"),
            P(),
            P(),
            P(),
            P("value"),
            P("value", None),
            P("dp", "value", None, None),
            P("dp", "value", None, None),
            P(),
            P(),
            P(),
        ),
        out_specs=P(None, "dp", "value"),
        check_vma=False,
    )
```

profile of v0, /device:TPU:0, one launch (start us, length us, event | category | flops | bytes accessed | tf_op | source)
XLA Modules:
  0.0 530.9 jit_solution(14495454870154887861)
XLA Ops:
  6.5 8.3 %copy.104 = f32[32,16,32,128]{3,2,1,0:T(8,128)} copy(f32[32,16,32,128]{3,2,1,0:T(8,128)} %param.25) | data formatting | bytes 16777216
  15.5 5.0 gather_fusion
  20.5 5.0 select_select_fusion.3
  25.6 8.3 %all-to-all-start = ((f32[16,16,32,128]{3,2,1,0:T(8,128)}), f32[16,16,32,128]{3,2,1,0:T(8,128)}, u32[]{:S(2)}, u32[]{:S(2)}) async-start(f32[16,16,32,128]{3,2,1,0:T(8,128)} %select_select_fusion.3), calls=%async_computation | async-start | bytes 8388608 | tf_op jit(solution)/shard_map/all_to_all | solution.py:99
  63.0 13.2 %all_gather.12 = bf16[32,4096]{1,0:T(8,128)(2,1)S(1)} all-gather(bf16[32,512]{1,0:T(8,128)(2,1)S(1)} %convolution_convert_fusion.3), channel_id=1, replica_groups=mesh['dp'=16,'value'=8] {'value'}, dimensions={1}, use_global_device_ids=true | all-gather | bytes 294912 | tf_op jit(solution)/shard_map/all_gather | solution.py:39
  76.3 4.0 copy.37
  80.4 5.0 gather_fusion.1
  85.3 12.8 %all_gather.13 = bf16[32,4096]{1,0:T(8,128)(2,1)S(1)} all-gather(bf16[32,512]{1,0:T(8,128)(2,1)S(1)} %convolution_convert_fusion.2), channel_id=1, replica_groups=mesh['dp'=16,'value'=8] {'value'}, dimensions={1}, use_global_device_ids=true | all-gather | bytes 294912 | tf_op jit(solution)/shard_map/all_gather | solution.py:39
  99.1 5.0 gather_fusion.2
  106.3 12.8 %all_gather.14 = bf16[32,4096]{1,0:T(8,128)(2,1)S(1)} all-gather(bf16[32,512]{1,0:T(8,128)(2,1)S(1)} %convolution_convert_fusion.1), channel_id=1, replica_groups=mesh['dp'=16,'value'=8] {'value'}, dimensions={1}, use_global_device_ids=true | all-gather | bytes 294912 | tf_op jit(solution)/shard_map/all_gather | solution.py:39
  119.8 13.0 %all_gather.15 = bf16[32,4096]{1,0:T(8,128)(2,1)S(1)} all-gather(bf16[32,512]{1,0:T(8,128)(2,1)S(1)} %convolution_convert_fusion), channel_id=1, replica_groups=mesh['dp'=16,'value'=8] {'value'}, dimensions={1}, use_global_device_ids=true | all-gather | bytes 294912 | tf_op jit(solution)/shard_map/all_gather | solution.py:39
  139.3 7.4 %all-to-all-start.1 = ((f32[16,16,32,128]{3,2,1,0:T(8,128)}), f32[16,16,32,128]{3,2,1,0:T(8,128)}, u32[]{:S(2)}, u32[]{:S(2)}) async-start(f32[16,16,32,128]{3,2,1,0:T(8,128)} %select_select_fusion.2), calls=%async_computation.2 | async-start | bytes 8388608 | tf_op jit(solution)/shard_map/all_to_all | solution.py:99
  153.5 5.0 select_select_fusion.1
  158.6 52.0 %all-to-all-done.1 = f32[16,16,32,128]{3,2,1,0:T(8,128)} async-done(((f32[16,16,32,128]{3,2,1,0:T(8,128)}), f32[16,16,32,128]{3,2,1,0:T(8,128)}, u32[]{:S(2)}, u32[]{:S(2)}) %all-to-all-start.1) | async-done | bytes 4194336 | tf_op jit(solution)/shard_map/all_to_all | solution.py:99
  210.6 17.6 %all-to-all-start.2 = ((f32[16,16,32,128]{3,2,1,0:T(8,128)}), f32[16,16,32,128]{3,2,1,0:T(8,128)}, u32[]{:S(2)}, u32[]{:S(2)}) async-start(f32[16,16,32,128]{3,2,1,0:T(8,128)} %select_select_fusion.1), calls=%async_computation.4 | async-start | bytes 8388608 | tf_op jit(solution)/shard_map/all_to_all | solution.py:99
  228.3 5.0 gather_fusion.3
  233.2 3.9 copy.41
  267.5 6.0 %multiply_reduce_fusion.7 = f32[32,16,32]{2,1,0:T(8,128)S(1)} fusion(f32[32,16,32,128]{3,2,1,0:T(8,128)} %dynamic-slice_dynamic-update-slice_fusion.6, f32[32,32,128]{2,1,0:T(8,128)S(1)} %bitcast.156, f32[32,32]{1,0:T(8,128)S(1)} %get-tuple-element.39), kind=kLoop, calls=%fused_computation.14 | loop fusion | flops 6275072 | bytes 8982528 | tf_op jit(solution)/shard_map/reduce_sum | solution.py:56
  276.2 13.6 %all-to-all-done.2 = f32[16,16,32,128]{3,2,1,0:T(8,128)} async-done(((f32[16,16,32,128]{3,2,1,0:T(8,128)}), f32[16,16,32,128]{3,2,1,0:T(8,128)}, u32[]{:S(2)}, u32[]{:S(2)}) %all-to-all-start.2) | async-done | bytes 4194336 | tf_op jit(solution)/shard_map/all_to_all | solution.py:99
  289.7 4.8 all-to-all-start.3
  295.8 7.8 %multiply_reduce_fusion.6 = (f32[32,16,32]{2,1,0:T(8,128)}, f32[32,16,32,128]{3,2,1,0:T(8,128)S(1)}) fusion(f32[32,32,128]{2,1,0:T(8,128)S(1)} %bitcast.175, f32[32,32,128]{2,1,0:T(8,128)S(1)} %bitcast.157, f32[32,16,32]{2,1,0:T(8,128)} %copy.39, f32[32,16,32,128]{3,2,1,0:T(8,128)} %dynamic-slice_dynamic-update-slice_fusion.6, f32[32,32]{1,0:T(8,128)S(1)} %get-tuple-element.39), kind=kLoop, calls=%fused_computation.12 | loop fusion | flops 10469376 | bytes 17960960 | tf_op jit(solution)/shard_map/reduce_sum | solution.py:59
  310.9 7.0 %multiply_reduce_fusion.4 = (f32[32,16,32]{2,1,0:T(8,128)}, f32[32,16,32,128]{3,2,1,0:T(8,128)S(1)}) fusion(f32[32,32,128]{2,1,0:T(8,128)S(1)} %bitcast.176, f32[32,32,128]{2,1,0:T(8,128)S(1)} %bitcast.159, f32[32,16,32]{2,1,0:T(8,128)S(1)} %copy.44, f32[32,16,32,128]{3,2,1,0:T(8,128)S(1)} %dynamic-slice_dynamic-update-slice_fusion.4, f32[32,32]{1,0:T(8,128)} %copy-done.26), kind=kLoop, calls=%fused_computation.9 | loop fusion | flops 10469376 | bytes 17960960 | tf_op jit(solution)/shard_map/reduce_sum | solution.py:59
  326.0 6.4 %multiply_reduce_fusion.2 = (f32[32,16,32]{2,1,0:T(8,128)}, f32[32,16,32,128]{3,2,1,0:T(8,128)}) fusion(f32[32,32,128]{2,1,0:T(8,128)S(1)} %bitcast.177, f32[32,32,128]{2,1,0:T(8,128)S(1)} %bitcast.161, f32[32,16,32]{2,1,0:T(8,128)S(1)} %copy.48, f32[32,16,32,128]{3,2,1,0:T(8,128)S(1)} %dynamic-slice_dynamic-update-slice_fusion.2, ...), kind=kLoop, calls=%fused_computation.6 | loop fusion | flops 10469376 | bytes 17960960 | tf_op jit(solution)/shard_map/reduce_sum | solution.py:59
  332.4 20.2 %all-to-all-done.3 = f32[16,16,32,128]{3,2,1,0:T(8,128)} async-done(((f32[16,16,32,128]{3,2,1,0:T(8,128)}), f32[16,16,32,128]{3,2,1,0:T(8,128)}, u32[]{:S(2)}, u32[]{:S(2)}) %all-to-all-start.3) | async-done | bytes 4194336 | tf_op jit(solution)/shard_map/all_to_all | solution.py:99
  357.4 6.0 %multiply_reduce_fusion.1 = f32[32,16,32]{2,1,0:T(8,128)S(1)} fusion(f32[32,16,32,128]{3,2,1,0:T(8,128)} %dynamic-slice_dynamic-update-slice_fusion, f32[32,32,128]{2,1,0:T(8,128)S(1)} %bitcast.154, f32[32,32]{1,0:T(8,128)S(1)} %get-tuple-element.33), kind=kLoop, calls=%fused_computation.5 | loop fusion | flops 6275072 | bytes 8982528 | tf_op jit(solution)/shard_map/reduce_sum | solution.py:56
  366.6 4.9 multiply_reduce_fusion
  371.7 24.0 %all-reduce = (f32[32,32]{1,0:T(8,128)S(1)}, f32[32,32]{1,0:T(8,128)S(1)}, f32[32,32]{1,0:T(8,128)S(1)}, f32[32,32]{1,0:T(8,128)S(1)}) all-reduce(f32[32,32]{1,0:T(8,128)S(1)} %multiply_reduce_fusion.8, f32[32,32]{1,0:T(8,128)S(1)} %multiply_reduce_fusion.11, ...), channel_id=1, replica_groups=mesh['dp'=16,'value'=8] {'value'}, use_global_device_ids=true, to_apply=%region_34.36 | all-reduce | flops 4096 | bytes 32768 | tf_op jit(solution)/shard_map/psum | solution.py:60
  410.5 3.4 fusion.6
  415.3 12.1 %reduce-scatter.5.cloned.1.call-done = f32[256,32]{0,1:T(8,128)} async-done(((f32[2048,32]{0,1:T(8,128)}), f32[256,32]{0,1:T(8,128)}) %reduce-scatter.5.cloned.1.call-update) | async-done | bytes 32784 | tf_op jit(solution)/shard_map/reduce_scatter | solution.py:64
  428.2 31.0 %reduce-scatter.7.cloned.1.call-done = f32[256,32]{0,1:T(8,128)} async-done(((f32[2048,32]{0,1:T(8,128)}), f32[256,32]{0,1:T(8,128)}) %reduce-scatter.7.cloned.1.call-update) | async-done | bytes 32784 | tf_op jit(solution)/shard_map/reduce_scatter | solution.py:64
  460.0 30.9 %reduce-scatter.9.cloned.1.call-done = f32[256,32]{0,1:T(8,128)} async-done(((f32[2048,32]{0,1:T(8,128)}), f32[256,32]{0,1:T(8,128)}) %reduce-scatter.9.cloned.1.call-update) | async-done | bytes 32784 | tf_op jit(solution)/shard_map/reduce_scatter | solution.py:64
  491.7 30.9 %reduce-scatter.11.cloned.1.call-done = f32[256,32]{0,1:T(8,128)} async-done(((f32[2048,32]{0,1:T(8,128)}), f32[256,32]{0,1:T(8,128)}) %reduce-scatter.11.cloned.1.call-update) | async-done | bytes 32784 | tf_op jit(solution)/shard_map/reduce_scatter | solution.py:64
  (223 shorter events, 94.0 us)
Async XLA Ops:
  6.5 392.9 %copy-start = (bf16[512,2048]{1,0:T(8,128)(2,1)S(1)}, bf16[512,2048]{1,0:T(8,128)(2,1)}, u32[]{:S(2)}) copy-start(bf16[512,2048]{1,0:T(8,128)(2,1)} %param.24) | copy-start | bytes 6291460
  25.6 11.5 %copy-start.31 = (s32[4,16,2]{1,2,0:T(2,128)S(1)}, s32[4,16,2]{1,2,0:T(2,128)}, u32[]{:S(2)}) copy-start(s32[4,16,2]{1,2,0:T(2,128)} %param.27) | copy-start | bytes 1540
  25.6 21.0 %copy-start.8 = (bf16[4,32,2048]{2,1,0:T(8,128)(2,1)S(1)}, bf16[4,32,2048]{2,1,0:T(8,128)(2,1)}, u32[]{:S(2)}) copy-start(bf16[4,32,2048]{2,1,0:T(8,128)(2,1)} %param.16) | copy-start | bytes 1572868
  25.6 113.7 %all-to-all-start = ((f32[16,16,32,128]{3,2,1,0:T(8,128)}), f32[16,16,32,128]{3,2,1,0:T(8,128)}, u32[]{:S(2)}, u32[]{:S(2)}) async-start(f32[16,16,32,128]{3,2,1,0:T(8,128)} %select_select_fusion.3), calls=%async_computation | async-start | bytes 8388608 | tf_op jit(solution)/shard_map/all_to_all | solution.py:99
  98.3 35.7 %copy-start.13 = (f32[4,8,16,128]{3,2,1,0:T(8,128)}, f32[4,8,16,128]{3,2,1,0:T(8,128)S(1)}, u32[]{:S(2)}) copy-start(f32[4,8,16,128]{3,2,1,0:T(8,128)S(1)} %copy.57) | copy-start | bytes 786436
  104.1 15.3 %copy-start.5 = (bf16[2048,512]{1,0:T(8,128)(2,1)S(1)}, bf16[2048,512]{1,0:T(8,128)(2,1)}, u32[]{:S(2)}) copy-start(bf16[2048,512]{1,0:T(8,128)(2,1)} %param.17) | copy-start | bytes 6291460
  119.2 15.0 %copy-start.14 = (f32[4,8,16,128]{3,2,1,0:T(8,128)S(1)}, f32[4,8,16,128]{3,2,1,0:T(8,128)}, u32[]{:S(2)}) copy-start(f32[4,8,16,128]{3,2,1,0:T(8,128)} %copy.58) | copy-start | bytes 786436
  119.2 17.2 %copy-start.7 = (f32[16,16,32,128]{3,2,1,0:T(8,128)S(1)}, f32[16,16,32,128]{3,2,1,0:T(8,128)}, u32[]{:S(2)}) copy-start(f32[16,16,32,128]{3,2,1,0:T(8,128)} %gather_fusion.1) | copy-start | bytes 12582916
  119.3 15.0 %copy-start.15 = (f32[4,8,16,128]{3,2,1,0:T(8,128)}, f32[4,8,16,128]{3,2,1,0:T(8,128)S(1)}, u32[]{:S(2)}) copy-start(f32[4,8,16,128]{3,2,1,0:T(8,128)S(1)} %copy.59) | copy-start | bytes 786436
  119.3 15.1 %copy-start.16 = (f32[4,8,16,128]{3,2,1,0:T(8,128)}, f32[4,8,16,128]{3,2,1,0:T(8,128)S(1)}, u32[]{:S(2)}) copy-start(f32[4,8,16,128]{3,2,1,0:T(8,128)S(1)} %copy.60) | copy-start | bytes 786436
  139.3 12.8 %copy-start.12 = (bf16[2048,64]{0,1:T(8,128)(2,1)S(1)}, bf16[2048,64]{0,1:T(8,128)(2,1)}, u32[]{:S(2)}) copy-start(bf16[2048,64]{0,1:T(8,128)(2,1)} %param.20) | copy-start | bytes 786436
  139.3 13.0 %copy-start.30 = (f32[32]{0:T(128)S(1)}, f32[32]{0:T(128)}, u32[]{:S(2)}) copy-start(f32[32]{0:T(128)} %param.22) | copy-start | bytes 388
  139.3 14.2 %copy-start.35 = (pred[16]{0:T(512)(128)(4,1)S(1)}, pred[16]{0:T(512)(128)(4,1)}, u32[]{:S(2)}) copy-start(pred[16]{0:T(512)(128)(4,1)} %compare_and_fusion.1) | copy-start | bytes 52
  139.3 71.3 %all-to-all-start.1 = ((f32[16,16,32,128]{3,2,1,0:T(8,128)}), f32[16,16,32,128]{3,2,1,0:T(8,128)}, u32[]{:S(2)}, u32[]{:S(2)}) async-start(f32[16,16,32,128]{3,2,1,0:T(8,128)} %select_select_fusion.2), calls=%async_computation.2 | async-start | bytes 8388608 | tf_op jit(solution)/shard_map/all_to_all | solution.py:99
  152.7 153.2 %copy-start.26 = (f32[32,32]{1,0:T(8,128)}, f32[32,32]{1,0:T(8,128)S(1)}, u32[]{:S(2)}) copy-start(f32[32,32]{1,0:T(8,128)S(1)} %get-tuple-element.37) | copy-start | bytes 12292
  158.6 69.7 %copy-start.36 = (s32[16]{0:T(128)S(1)}, s32[16]{0:T(128)}, u32[]{:S(2)}) copy-start(s32[16]{0:T(128)} %compare_select_fusion.4) | copy-start | bytes 196
  210.6 79.1 %all-to-all-start.2 = ((f32[16,16,32,128]{3,2,1,0:T(8,128)}), f32[16,16,32,128]{3,2,1,0:T(8,128)}, u32[]{:S(2)}, u32[]{:S(2)}) async-start(f32[16,16,32,128]{3,2,1,0:T(8,128)} %select_select_fusion.1), calls=%async_computation.4 | async-start | bytes 8388608 | tf_op jit(solution)/shard_map/all_to_all | solution.py:99
  233.2 27.7 %copy-start.33 = (pred[16]{0:T(512)(128)(4,1)S(1)}, pred[16]{0:T(512)(128)(4,1)}, u32[]{:S(2)}) copy-start(pred[16]{0:T(512)(128)(4,1)} %get-tuple-element.10) | copy-start | bytes 52
  233.2 27.7 %copy-start.34 = (pred[16]{0:T(512)(128)(4,1)S(1)}, pred[16]{0:T(512)(128)(4,1)}, u32[]{:S(2)}) copy-start(pred[16]{0:T(512)(128)(4,1)} %compare_and_fusion) | copy-start | bytes 52
  247.2 13.8 %copy-start.6 = (f32[16,16,32,128]{3,2,1,0:T(8,128)S(1)}, f32[16,16,32,128]{3,2,1,0:T(8,128)}, u32[]{:S(2)}) copy-start(f32[16,16,32,128]{3,2,1,0:T(8,128)} %gather_fusion.3) | copy-start | bytes 12582916
  289.7 62.9 %all-to-all-start.3 = ((f32[16,16,32,128]{3,2,1,0:T(8,128)}), f32[16,16,32,128]{3,2,1,0:T(8,128)}, u32[]{:S(2)}, u32[]{:S(2)}) async-start(f32[16,16,32,128]{3,2,1,0:T(8,128)} %select_select_fusion), calls=%async_computation.6 | async-start | bytes 8388608 | tf_op jit(solution)/shard_map/all_to_all | solution.py:99
  294.6 132.9 %reduce-scatter.5.cloned.1.call-start = ((), (), s32[]{:S(2)}) async-start(), calls=%async_computation.8 | async-start | bytes 294912 | tf_op jit(solution)/shard_map/reduce_scatter | solution.py:64
  295.8 9.7 %copy-start.21 = (f32[32,16,128]{2,1,0:T(8,128)S(1)}, f32[32,16,128]{2,1,0:T(8,128)}, u32[]{:S(2)}) copy-start(f32[32,16,128]{2,1,0:T(8,128)} %broadcast_multiply_fusion.2) | copy-start | bytes 786436
  310.9 8.9 %copy-start.20 = (f32[32,16,128]{2,1,0:T(8,128)S(1)}, f32[32,16,128]{2,1,0:T(8,128)}, u32[]{:S(2)}) copy-start(f32[32,16,128]{2,1,0:T(8,128)} %broadcast_multiply_fusion.1) | copy-start | bytes 786436
  352.6 10.8 %copy-start.28 = (f32[32,32]{1,0:T(8,128)S(1)}, f32[32,32]{1,0:T(8,128)}, u32[]{:S(2)}) copy-start(f32[32,32]{1,0:T(8,128)} %get-tuple-element.32) | copy-start | bytes 12292
  357.3 8.9 %copy-start.18 = (f32[32,16,128]{2,1,0:T(8,128)S(1)}, f32[32,16,128]{2,1,0:T(8,128)}, u32[]{:S(2)}) copy-start(f32[32,16,128]{2,1,0:T(8,128)} %multiply_multiply_fusion) | copy-start | bytes 786436
  357.3 9.2 %copy-start.1 = (f32[32,16,32,128]{3,2,1,0:T(8,128)S(1)}, f32[32,16,32,128]{3,2,1,0:T(8,128)}, u32[]{:S(2)}) copy-start(f32[32,16,32,128]{3,2,1,0:T(8,128)} %dynamic-slice_dynamic-update-slice_fusion) | copy-start | bytes 25165828
  366.6 29.2 %copy-start.9 = (bf16[4,32,2048]{2,1,0:T(8,128)(2,1)S(1)}, bf16[4,32,2048]{2,1,0:T(8,128)(2,1)}, u32[]{:S(2)}) copy-start(bf16[4,32,2048]{2,1,0:T(8,128)(2,1)} %param.16) | copy-start | bytes 1572868
  366.6 29.2 %copy-start.38 = (f32[16]{0:T(128)S(1)}, f32[16]{0:T(128)}, u32[]{:S(2)}) copy-start(f32[16]{0:T(128)} %param.23) | copy-start | bytes 196
  400.6 58.6 %reduce-scatter.7.cloned.1.call-start = ((), (), s32[]{:S(2)}) async-start(), calls=%async_computation.9 | async-start | bytes 294912 | tf_op jit(solution)/shard_map/reduce_scatter | solution.py:64
  405.5 85.4 %reduce-scatter.9.cloned.1.call-start = ((), (), s32[]{:S(2)}) async-start(), calls=%async_computation.10 | async-start | bytes 294912 | tf_op jit(solution)/shard_map/reduce_scatter | solution.py:64
  410.4 112.2 %reduce-scatter.11.cloned.1.call-start = ((), (), s32[]{:S(2)}) async-start(), calls=%async_computation.11 | async-start | bytes 294912 | tf_op jit(solution)/shard_map/reduce_scatter | solution.py:64
  (15 other events, 77.8 us)
Sparse Core Ops, SparseCore 0:
  400.8 26.6 reduce-scatter.4
  429.9 29.2 reduce-scatter.6
  461.6 29.3 reduce-scatter.8
  493.3 29.3 reduce-scatter.10
where the time goes:
time: 541 us; the launch traced here: 531 us
  waiting for transfers between devices  191 us (35%)
  other arithmetic  86.4 us (16%)
  blocking collectives  75.9 us (14%)
  local copies, waits for them, and re-layouts  60.3 us (11%)
  between operations  44.6 us (8%)
  starting transfers between devices  38.3 us (7%)
  matrix products  34.6 us (6%)
    reduce_scatter x4, waiting for transfers between devices, advance(): lax.psum_scatter(lax.dot_general(out_weight, gated, (((0,), (1,)), ((), (...  105 us
    all_to_all x4, waiting for transfers between devices, on_device(): lax.all_to_all(outgoing, 'dp', split_axis=0, concat_axis=0, tiled=True)  85.7 us
    all_gather x4, blocking collectives, advance(): lax.all_gather(joined, 'value', axis=1, tiled=True).astype(jnp.float32)  51.8 us
    all_to_all x4, starting transfers between devices, on_device(): lax.all_to_all(outgoing, 'dp', split_axis=0, concat_axis=0, tiled=True)  38.1 us
    reduce_sum x4, other arithmetic, advance(): readout = jnp.sum(states * queries[:, None], axis=-1)  26 us
    psum x1, blocking collectives, advance(): squares = lax.psum(jnp.sum(readout * readout, axis=1), 'value')  24 us
    gather x4, local copies, waits for them, and re-layouts, outgoing_states(): picked = jnp.take(prefilled, chosen, axis=0)  19.9 us
    unnamed x93, local copies, waits for them, and re-layouts  18.4 us
  transfers between devices with their start and end apart: 8, of which 7 were waited for; matrix products, arithmetic and copies ran while one was open for 26% of the time, Pallas kernels for 0%

commit v1 on v0

v1 whole, which is shorter than its diff:
```python
import functools

import jax
import jax.numpy as jnp
from jax import lax
from jax.experimental import pallas as pl
from jax.experimental.pallas import tpu as pltpu
from jax.sharding import PartitionSpec as P

F32 = jnp.float32
BF16 = jnp.bfloat16
MESH = pl.DeviceIdType.MESH

STEPS = 4
REPLACED = 2
N_DP = 16
N_VALUE = 8
N_X = 4
ROWS = 32
H = 32
DK = 128
DV = 128
WIDTH = 2048
COLS = 512
PIECE = 256
BLOCKS = ROWS + N_DP
HEADS = 4
TILE = HEADS * STEPS
GROUPS = COLS // 128

FIRST, LAST, FOREIGN = 0, 1, 2
BASE = (0, 16, 32)
CHUNK = 16


def iota(shape, dim):
    return lax.broadcasted_iota(jnp.int32, shape, dim)


def dot(a, b, **kw):
    return jnp.dot(a, b, preferred_element_type=F32, **kw)


def dot_t(a, b):
    return lax.dot_general(a, b, (((1,), (1,)), ((), ())), preferred_element_type=F32)


def kernel(
    fin_ref,
    own_ref,
    slot_ref,
    logd_ref,
    bias_ref,
    gain_ref,
    x_hbm,
    wqk_hbm,
    wv_hbm,
    wg_hbm,
    wr_hbm,
    wo_hbm,
    st_hbm,
    pf_hbm,
    out_ref,
    x_v,
    wqk_v,
    wv_v,
    wg_v,
    wr_v,
    wo_v,
    st_v,
    pf_v,
    zf,
    snd_f,
    gbuf,
    msc,
    rsnd,
    rrcv,
    rf,
    val_s,
    gate_s,
    gat_s,
    sqbuf,
    r1_snd,
    r1_rcv,
    part,
    r2_snd,
    r2_rcv,
    loc,
    ag_s,
    ag_r,
    fs,
    fr,
    bs,
    br,
    qs,
    qr,
    r1s,
    r1r,
    r2s,
    r2r,
):
    me_d = lax.axis_index("dp")
    me_v = lax.axis_index("value")
    x = me_v // 2
    c = me_v % 2
    xr, xl, xo = (x + 1) % N_X, (x + 3) % N_X, (x + 2) % N_X

    def vid(xx, cc):
        return xx * 2 + cc

    right, left, partner = vid(xr, c), vid(xl, c), vid(x, 1 - c)

    def load(src, dst, k):
        cp = pltpu.make_async_copy(src, dst, loc.at[k])
        cp.start()
        return cp

    l_x = load(x_hbm, x_v, 0)
    l_qk = load(wqk_hbm, wqk_v, 1)

    barrier = pltpu.get_barrier_semaphore()
    for i in range(1, N_DP):
        pl.semaphore_signal(barrier, inc=1, device_id=((me_d + i) % N_DP, me_v), device_id_type=MESH)
    for i in range(1, N_VALUE):
        pl.semaphore_signal(barrier, inc=1, device_id=(me_d, (me_v + i) % N_VALUE), device_id_type=MESH)

    l_x.wait()
    l_qk.wait()
    l_r = load(wr_hbm, wr_v, 2)
    l_v = load(wv_hbm, wv_v, 3)
    l_g = load(wg_hbm, wg_v, 4)
    l_p = load(pf_hbm, pf_v, 5)
    l_s0 = load(st_hbm.at[pl.ds(0, 16)], st_v.at[pl.ds(0, 16)], 6)
    l_s1 = load(st_hbm.at[pl.ds(16, 16)], st_v.at[pl.ds(16, 16)], 7)
    l_o = load(wo_hbm, wo_v, 8)
    xin = x_v[...].reshape(STEPS * ROWS, WIDTH)
    joined = dot(xin, wqk_v[...]).astype(BF16)
    joined_f = joined.astype(F32)
    pick = jnp.zeros((N_DP, ROWS), F32)
    for t in range(STEPS):
        for j in range(REPLACED):
            hit = (iota((N_DP, ROWS), 0) == own_ref[t, me_d, j]) & (iota((N_DP, ROWS), 1) == fin_ref[t, me_d, j])
            pick = jnp.where(hit, 1.0, pick)
    pick = pick.astype(BF16)
    for t in range(STEPS):
        chosen = dot(pick, joined[t * ROWS : (t + 1) * ROWS])
        for h in range(HEADS):
            at = (h * STEPS + t) * BLOCKS
            zf[at : at + ROWS] = joined_f[t * ROWS : (t + 1) * ROWS, h * 128 : (h + 1) * 128]
            zf[at + ROWS : at + BLOCKS] = chosen[:, h * 128 : (h + 1) * 128]

    def block_of(r):
        return zf[pl.ds(r, TILE, stride=BLOCKS), :].astype(BF16)

    for o in range(N_DP):
        snd_f[o] = block_of(ROWS + o)
    pl.semaphore_wait(barrier, N_DP + N_VALUE - 2)

    def foreign(i):
        dst = (me_d + i) % N_DP
        return pltpu.make_async_remote_copy(
            src_ref=snd_f.at[dst],
            dst_ref=gbuf.at[me_v, ROWS + me_d],
            send_sem=fs.at[i],
            recv_sem=fr.at[i],
            device_id=(dst, me_v),
            device_id_type=MESH,
        )

    for i in range(1, N_DP):
        foreign(i).start()
    gbuf[me_v, ROWS + me_d] = snd_f[me_d]
    for r in range(CHUNK):
        gbuf[me_v, r] = block_of(r)

    def hop(chunk, k):
        slot, half, to = (
            (me_v, None, right),
            (me_v, None, left),
            (me_v, None, partner),
            (left, 0, right),
            (right, 1, left),
            (left, None, partner),
            (right, None, partner),
            (vid(xo, c), 0, partner),
            (vid(xo, c), 1, partner),
        )[k]
        return ag_copy(chunk, k, slot, half, to)

    def ag_copy(chunk, k, slot, half, to):
        rows = pl.ds(BASE[chunk], CHUNK) if half is None else pl.ds(BASE[chunk] + half * 8, 8)
        return pltpu.make_async_remote_copy(
            src_ref=gbuf.at[slot, rows],
            dst_ref=gbuf.at[slot, rows],
            send_sem=ag_s.at[chunk, k],
            recv_sem=ag_r.at[chunk, k],
            device_id=(me_d, to),
            device_id_type=MESH,
        )

    def arrived(chunk, k):
        slot, half = (
            (left, None),
            (right, None),
            (partner, None),
            (vid(xo, c), 0),
            (vid(xo, c), 1),
            (vid(xl, 1 - c), None),
            (vid(xr, 1 - c), None),
            (vid(xo, 1 - c), 0),
            (vid(xo, 1 - c), 1),
        )[k]
        ag_copy(chunk, k, slot, half, partner).wait_recv()

    def send_own(chunk):
        for k in range(3):
            hop(chunk, k).start()

    def forward_near(chunk):
        arrived(chunk, 0)
        hop(chunk, 3).start()
        hop(chunk, 5).start()
        arrived(chunk, 1)
        hop(chunk, 4).start()
        hop(chunk, 6).start()

    def forward_far(chunk):
        arrived(chunk, 3)
        hop(chunk, 7).start()
        arrived(chunk, 4)
        hop(chunk, 8).start()

    def all_here(chunk):
        for k in (2, 5, 6, 7, 8):
            arrived(chunk, k)

    send_own(FIRST)
    for r in range(CHUNK, 2 * CHUNK):
        gbuf[me_v, r] = block_of(r)
    l_r.wait()
    rates = dot(xin, wr_v[...])
    for i in range(1, N_DP):
        foreign(i).wait_recv()
    send_own(FOREIGN)
    send_own(LAST)
    l_v.wait()
    val_s[...] = dot(xin, wv_v[...])
    forward_near(FIRST)
    l_g.wait()
    gate_s[...] = dot(xin, wg_v[...])
    forward_far(FIRST)
    forward_near(FOREIGN)

    lane = iota((8, 128), 1)
    sub = iota((8, 128), 0)
    state_masks = [(lane % H) // 2 == 2 * i + sub // 4 for i in range(8)]
    gram_masks = [(lane % 64) // 4 == 2 * i + sub // 4 for i in range(8)]

    def diagonal(full, masks):
        sums = []
        for kind in range(2):
            acc = jnp.zeros((8, 128), F32)
            for i in range(8):
                at = kind * 64 + i * 8
                acc = jnp.where(masks[i], full[at : at + 8], acc)
            sums.append(acc + pltpu.roll(acc, 4, 0))
        return jnp.where(sub < 4, sums[0], sums[1])

    def contract(qk, state):
        full = dot_t(qk, state.reshape(COLS, DK).astype(BF16))
        return [diagonal(full[:, g * 128 : (g + 1) * 128], state_masks) for g in range(GROUPS)]

    def own_rows(first, count):
        def one(r, _):
            qk = gbuf[:, r].reshape(N_VALUE * TILE, DK)
            at = pl.multiple_of(r * 8, 8)
            for g, block in enumerate(contract(qk, st_v[r])):
                msc[g, pl.ds(at, 8)] = block
            msc[GROUPS, pl.ds(at, 8)] = diagonal(dot_t(qk, qk), gram_masks)
            return 0

        def two(i, _):
            one(first + 2 * i, 0)
            one(first + 2 * i + 1, 0)
            return 0

        lax.fori_loop(0, count // 2, two, 0)

    def foreign_rows():
        def one(d):
            slot = jnp.int32(0)
            for t in range(STEPS):
                for j in range(REPLACED):
                    slot = jnp.where(own_ref[t, d, j] == me_d, slot_ref[t, d, j], slot)
            qk = gbuf[:, ROWS + d].reshape(N_VALUE * TILE, DK)
            blocks = contract(qk, pf_v[slot])
            rsnd[d] = jnp.concatenate(blocks, axis=0).astype(BF16)

        def two(i, _):
            one(2 * i)
            one(2 * i + 1)
            return 0

        lax.fori_loop(0, N_DP // 2, two, 0)

    def back(i):
        dst = (me_d + i) % N_DP
        return pltpu.make_async_remote_copy(
            src_ref=rsnd.at[dst],
            dst_ref=rrcv.at[me_d],
            send_sem=bs.at[i],
            recv_sem=br.at[i],
            device_id=(dst, me_v),
            device_id_type=MESH,
        )

    all_here(FIRST)
    l_s0.wait()
    own_rows(0, CHUNK)
    forward_far(FOREIGN)
    forward_near(LAST)
    all_here(FOREIGN)
    l_p.wait()
    foreign_rows()
    for i in range(1, N_DP):
        back(i).start()
    rrcv[me_d] = rsnd[me_d]
    forward_far(LAST)
    all_here(LAST)
    l_s1.wait()
    own_rows(CHUNK, CHUNK)

    gram = [msc[GROUPS, pl.ds(k, ROWS, stride=8), :] for k in range(2 * STEPS)]
    src = iota((DK, 128), 0)
    head = (iota((DK, 128), 1) % H) // 2
    spread = [(src == 64 + head * 4 + s).astype(F32) for s in range(STEPS)]
    exact = dict(precision=lax.Precision.HIGHEST)
    by_key = dot(jnp.concatenate(gram, axis=0), jnp.concatenate(spread, axis=1), **exact)
    inv_k, inv_q = [], []
    for t in range(STEPS):
        kk = by_key[(STEPS + t) * ROWS : (STEPS + t + 1) * ROWS, t * 128 : (t + 1) * 128]
        qq = dot(gram[t], (src == head * 4 + t).astype(F32), **exact)
        inv_k.append(lax.rsqrt(kk + 1e-06))
        inv_q.append(lax.rsqrt(qq + 1e-06) * DK ** (-0.5))

    def key_key(s, t):
        return by_key[(STEPS + t) * ROWS : (STEPS + t + 1) * ROWS, s * 128 : (s + 1) * 128] * (inv_k[s] * inv_k[t])

    def key_query(s, t):
        return by_key[t * ROWS : (t + 1) * ROWS, s * 128 : (s + 1) * 128] * (inv_k[s] * inv_q[t])

    seg = iota((1, 128), 1) // H
    in_seg = iota((1, 128), 1) % H
    decay = jnp.zeros((1, 128), F32)
    bias = jnp.zeros((1, 128), F32)
    for h in range(H):
        decay = jnp.where(in_seg == h, logd_ref[h], decay)
        bias = jnp.where(in_seg == h, bias_ref[h], bias)
    wide = jnp.concatenate([rates, rates], axis=1)
    turned = pltpu.roll(wide, H, 1)
    odd = seg % 2 == 1
    strength = jax.nn.sigmoid(jnp.where(odd, turned, wide))
    retain = jnp.exp(-jnp.exp(decay) * jax.nn.softplus(jnp.where(odd, wide, turned) + bias))

    row = iota((ROWS, 128), 0)
    row_o = iota((ROWS, N_DP), 0)
    latest = jnp.full((ROWS, N_DP), -1, jnp.int32)
    owner_of = jnp.full((ROWS, 128), -1, jnp.int32)
    fresh, replaced, takes = [], [], []
    for t in range(STEPS):
        hit = jnp.zeros((ROWS, 128), jnp.bool_)
        for j in range(REPLACED):
            done, owner = fin_ref[t, me_d, j], own_ref[t, me_d, j]
            hit = hit | (row == done)
            latest = jnp.where(row_o == done, owner, latest)
            owner_of = jnp.where(row == done, owner, owner_of)
        fresh.append(hit)
        replaced.append(owner_of >= 0)
        takes.append((latest == iota((ROWS, N_DP), 1)).astype(BF16))

    for i in range(1, N_DP):
        back(i).wait_recv()
    rf[...] = rrcv[...].astype(F32).reshape(N_DP * GROUPS * 8, 128)
    returned = []
    for k in range(2 * STEPS):
        parts = [rf[pl.ds(g * 8 + k, N_DP, stride=GROUPS * 8), :] for g in range(GROUPS)]
        returned.append(dot(takes[k % STEPS], jnp.concatenate(parts, axis=1).astype(BF16)))

    readouts = [[None] * GROUPS for _ in range(STEPS)]
    squares = [None] * STEPS
    kks = {(s, t): key_key(s, t) for t in range(STEPS) for s in range(t)}
    kqs = {(s, t): key_query(s, t) for t in range(STEPS) for s in range(t + 1)}
    for g in range(GROUPS):
        lanes = slice(g * 128, (g + 1) * 128)
        written = []
        kept = None
        for t in range(STEPS):
            rows = slice(t * ROWS, (t + 1) * ROWS)
            a, b = retain[rows], strength[rows]
            kept = a if kept is None else jnp.where(fresh[t], a, kept * a)
            written = [jnp.where(fresh[t], 0.0, w * a) for w in written]

            def base(k):
                mine = msc[g, pl.ds(k, ROWS, stride=8), :]
                return jnp.where(replaced[t], returned[k][:, lanes], mine)

            memory = kept * base(STEPS + t) * inv_k[t]
            readout = kept * base(t) * inv_q[t]
            for s, w in enumerate(written):
                memory = memory + w * kks[s, t]
                readout = readout + w * kqs[s, t]
            update = (val_s[rows, lanes] - memory) * b
            readout = readout + update * kqs[t, t]
            written.append(update)
            readouts[t][g] = readout
            square = readout * readout
            squares[t] = square if g == 0 else squares[t] + square
    packed = jnp.zeros((ROWS, 128), F32)
    for t in range(STEPS):
        total = squares[t] + pltpu.roll(squares[t], 64, 1)
        total = total + pltpu.roll(total, 32, 1)
        packed = jnp.where(seg == t, total, packed)
    sqbuf[me_v] = packed.astype(BF16)

    def square_copy(i):
        return pltpu.make_async_remote_copy(
            src_ref=sqbuf.at[me_v],
            dst_ref=sqbuf.at[me_v],
            send_sem=qs.at[i],
            recv_sem=qr.at[i],
            device_id=(me_d, (me_v + i) % N_VALUE),
            device_id_type=MESH,
        )

    def square_here(i):
        origin = (me_v + N_VALUE - i) % N_VALUE
        pltpu.make_async_remote_copy(
            src_ref=sqbuf.at[origin],
            dst_ref=sqbuf.at[origin],
            send_sem=qs.at[i],
            recv_sem=qr.at[i],
            device_id=(me_d, (me_v + i) % N_VALUE),
            device_id_type=MESH,
        ).wait_recv()

    for i in range(1, N_VALUE):
        square_copy(i).start()
    for g in range(GROUPS):
        gain = jnp.zeros((1, 128), F32)
        for e in range(4):
            gain = jnp.where(seg == e, gain_ref[g * 4 + e], gain)
        for t in range(STEPS):
            gating = gate_s[t * ROWS : (t + 1) * ROWS, g * 128 : (g + 1) * 128]
            readouts[t][g] = readouts[t][g] * gain * (gating * jax.nn.sigmoid(gating))
    for i in range(1, N_VALUE):
        square_here(i)
    summed = jnp.sum(sqbuf[...].astype(F32), axis=0)
    for t in range(STEPS):
        total = jnp.where(seg == t, summed, 0.0)
        total = total + pltpu.roll(total, 64, 1)
        total = total + pltpu.roll(total, 32, 1)
        scaling = lax.rsqrt(total * (1.0 / DV) + 1e-06)
        for g in range(GROUPS):
            gat_s[t * ROWS : (t + 1) * ROWS, g * 128 : (g + 1) * 128] = (readouts[t][g] * scaling).astype(BF16)

    l_o.wait()
    gated = gat_s[...]
    order = (xo, xr, xl, x)

    def project(to):
        at = pl.multiple_of(to * PIECE, PIECE)
        return dot(gated, wo_v[:, pl.ds(at, PIECE)])

    def first_copy(k):
        return pltpu.make_async_remote_copy(
            src_ref=r1_snd.at[k],
            dst_ref=r1_rcv.at[k],
            send_sem=r1s.at[k],
            recv_sem=r1r.at[k],
            device_id=(me_d, partner),
            device_id_type=MESH,
        )

    def second_copy(k):
        return pltpu.make_async_remote_copy(
            src_ref=r2_snd.at[k],
            dst_ref=r2_rcv.at[k],
            send_sem=r2s.at[k],
            recv_sem=r2r.at[k],
            device_id=(me_d, vid(order[k], c)),
            device_id_type=MESH,
        )

    for k in range(N_X):
        r1_snd[k] = project(vid(order[k], 1 - c)).astype(BF16)
        first_copy(k).start()
    for k in range(N_X):
        part[k] = project(vid(order[k], c))
    for k in range(N_X - 1):
        first_copy(k).wait_recv()
        r2_snd[k] = (part[k] + r1_rcv[k].astype(F32)).astype(BF16)
        second_copy(k).start()
    first_copy(3).wait_recv()
    total = part[3] + r1_rcv[3].astype(F32)
    for k in (1, 2, 0):
        second_copy(k).wait_recv()
        total = total + r2_rcv[k].astype(F32)
    out_ref[...] = total.astype(BF16)

    for i in range(1, N_DP):
        foreign(i).wait_send()
        back(i).wait_send()
    for chunk in range(3):
        for k in range(9):
            hop(chunk, k).wait_send()
    for i in range(1, N_VALUE):
        square_copy(i).wait_send()
    for k in range(N_X):
        first_copy(k).wait_send()
    for k in range(N_X - 1):
        second_copy(k).wait_send()


def on_device(
    inputs,
    qk_weight,
    value_weight,
    output_gate_weight,
    rate_weight,
    log_decay,
    decay_bias,
    norm_gain,
    out_weight,
    states,
    prefilled,
    finished,
    new_owner,
    new_slot,
):
    smem = pl.BlockSpec(memory_space=pltpu.SMEM)
    hbm = pl.BlockSpec(memory_space=pl.ANY)
    dma = pltpu.SemaphoreType.DMA
    produced = pl.pallas_call(
        kernel,
        out_shape=jax.ShapeDtypeStruct((STEPS * ROWS, PIECE), BF16),
        in_specs=[smem] * 6 + [hbm] * 8,
        out_specs=pl.BlockSpec(memory_space=pltpu.VMEM),
        scratch_shapes=[
            pltpu.VMEM((STEPS, ROWS, WIDTH), BF16),
            pltpu.VMEM((WIDTH, COLS), BF16),
            pltpu.VMEM((WIDTH, COLS), BF16),
            pltpu.VMEM((WIDTH, COLS), BF16),
            pltpu.VMEM((WIDTH, 2 * H), BF16),
            pltpu.VMEM((COLS, WIDTH), BF16),
            pltpu.VMEM((ROWS, 16, H, DK), F32),
            pltpu.VMEM((16, 16, H, DK), F32),
            pltpu.VMEM((TILE * BLOCKS, DK), F32),
            pltpu.VMEM((N_DP, TILE, DK), BF16),
            pltpu.VMEM((N_VALUE, BLOCKS, TILE, DK), BF16),
            pltpu.VMEM((GROUPS + 1, ROWS * 8, 128), F32),
            pltpu.VMEM((N_DP, GROUPS * 8, 128), BF16),
            pltpu.VMEM((N_DP, GROUPS * 8, 128), BF16),
            pltpu.VMEM((N_DP * GROUPS * 8, 128), F32),
            pltpu.VMEM((STEPS * ROWS, COLS), F32),
            pltpu.VMEM((STEPS * ROWS, COLS), F32),
            pltpu.VMEM((STEPS * ROWS, COLS), BF16),
            pltpu.VMEM((N_VALUE, ROWS, 128), BF16),
            pltpu.VMEM((N_X, STEPS * ROWS, PIECE), BF16),
            pltpu.VMEM((N_X, STEPS * ROWS, PIECE), BF16),
            pltpu.VMEM((N_X, STEPS * ROWS, PIECE), F32),
            pltpu.VMEM((N_X - 1, STEPS * ROWS, PIECE), BF16),
            pltpu.VMEM((N_X - 1, STEPS * ROWS, PIECE), BF16),
            dma((9,)),
            dma((3, 9)),
            dma((3, 9)),
            dma((N_DP,)),
            dma((N_DP,)),
            dma((N_DP,)),
            dma((N_DP,)),
            dma((N_VALUE,)),
            dma((N_VALUE,)),
            dma((N_X,)),
            dma((N_X,)),
            dma((N_X - 1,)),
            dma((N_X - 1,)),
        ],
        compiler_params=pltpu.CompilerParams(
            collective_id=0, has_side_effects=True, vmem_limit_bytes=56 * 2**20
        ),
        name="delta_steps",
    )(
        finished,
        new_owner,
        new_slot,
        log_decay,
        decay_bias,
        norm_gain,
        inputs,
        qk_weight,
        value_weight,
        output_gate_weight,
        rate_weight,
        out_weight,
        states,
        prefilled,
    )
    return produced.reshape(STEPS, ROWS, PIECE)


def solution(mesh):
    return jax.shard_map(
        on_device,
        mesh=mesh,
        in_specs=(
            P(None, "dp", None),
            P(None, "value"),
            P(None, "value"),
            P(None, "value"),
            P(),
            P(),
            P(),
            P("value"),
            P("value", None),
            P("dp", "value", None, None),
            P("dp", "value", None, None),
            P(),
            P(),
            P(),
        ),
        out_specs=P(None, "dp", "value"),
        check_vma=False,
    )
```

time: 541 us -> 53 us (0.10)
  the two profiles are of different devices: /device:TPU:0 before, /device:TPU:1 now
where the time goes in v1:
time: 53 us; the launch traced here: 52.5 us
  Pallas kernels  45 us (85%)
  local copies, waits for them, and re-layouts  7.58 us (14%)
    pallas_call x1, Pallas kernels, on_device(): pl.pallas_call(kernel, out_shape=jax.ShapeDtypeStruct((STEPS * ROWS, PIEC...  45 us
    unnamed x5, local copies, waits for them, and re-layouts  7.58 us

profile of v1, /device:TPU:1, one launch (start us, length us, event | category | flops | bytes accessed | tf_op | source)
XLA Modules:
  0.0 52.5 jit_solution(3231532368850872152)
XLA Ops:
  0.0 1.4 %copy.15.fin_ref = s32[4,16,2]{2,1,0:T(8,128)} copy(s32[4,16,2]{1,2,0:T(2,128)} %param.25) | data formatting | bytes 1024 | tf_op args[11]
  1.4 1.4 %copy.16.own_ref = s32[4,16,2]{2,1,0:T(8,128)} copy(s32[4,16,2]{1,2,0:T(2,128)} %param.26) | data formatting | bytes 1024 | tf_op args[12]
  2.8 1.4 %copy.17.slot_ref = s32[4,16,2]{2,1,0:T(8,128)} copy(s32[4,16,2]{1,2,0:T(2,128)} %param.27) | data formatting | bytes 1024 | tf_op args[13]
  4.2 1.9 %copy.18.wr_hbm = bf16[2048,64]{1,0:T(8,128)(2,1)} copy(bf16[2048,64]{0,1:T(8,128)(2,1)} %param.18) | data formatting | bytes 524288 | tf_op args[4]
  6.1 45.0 %delta_steps.1 = bf16[128,256]{1,0:T(8,128)(2,1)} custom-call(s32[4,16,2]{2,1,0:T(8,128)} %copy.15.fin_ref, s32[4,16,2]{2,1,0:T(8,128)} %copy.16.own_ref, s32[4,16,2]{2,1,0:T(8,128)} %copy.17.slot_ref, f32[32]{0:T(128)} %logd_ref.1, f32[32]{0:T(128)} %bias_ref.1, f32[16]{0:T(128)} %gain_ref.1, bf16[4,32,2048]{2,1,0:T(8,128)(2,1)} %x_hbm.1, ...), custom_call_target="tpu_custom_call" | custom-call | tf_op jit(solution)/shard_map/delta_steps/pallas_call | solution.py:543
  51.1 1.5 %copy.20 = bf16[4,32,256]{2,1,0:T(8,128)(2,1)} copy(bf16[4,32,256]{2,1,0:T(8,128)(2,1)} %bitcast.1) | data formatting | bytes 131072

commit v2 on v1

--- a/solution.py
+++ b/solution.py
@@ -28,8 +28,8 @@
 TILE = HEADS * STEPS
 GROUPS = COLS // 128
 
-FIRST, LAST, FOREIGN = 0, 1, 2
-BASE = (0, 16, 32)
+FIRST, LAST = 0, 1
+BASE = (0, 16)
 CHUNK = 16
 
 
@@ -46,12 +46,12 @@
 
 
 def kernel(
-    fin_ref,
-    own_ref,
-    slot_ref,
-    logd_ref,
-    bias_ref,
-    gain_ref,
+    fin_hbm,
+    own_hbm,
+    slot_hbm,
+    logd_hbm,
+    bias_hbm,
+    gain_hbm,
     x_hbm,
     wqk_hbm,
     wv_hbm,
@@ -61,6 +61,12 @@
     st_hbm,
     pf_hbm,
     out_ref,
+    fin_ref,
+    own_ref,
+    slot_ref,
+    logd_ref,
+    bias_ref,
+    gain_ref,
     x_v,
     wqk_v,
     wv_v,
@@ -90,6 +96,8 @@
     ag_r,
     fs,
     fr,
+    fps,
+    fpr,
     bs,
     br,
     qs,
@@ -117,29 +125,46 @@
 
     l_x = load(x_hbm, x_v, 0)
     l_qk = load(wqk_hbm, wqk_v, 1)
-
-    barrier = pltpu.get_barrier_semaphore()
-    for i in range(1, N_DP):
-        pl.semaphore_signal(barrier, inc=1, device_id=((me_d + i) % N_DP, me_v), device_id_type=MESH)
-    for i in range(1, N_VALUE):
-        pl.semaphore_signal(barrier, inc=1, device_id=(me_d, (me_v + i) % N_VALUE), device_id_type=MESH)
-
-    l_x.wait()
-    l_qk.wait()
+    scalars = (
+        (fin_hbm, fin_ref),
+        (own_hbm, own_ref),
+        (slot_hbm, slot_ref),
+        (logd_hbm, logd_ref),
+        (bias_hbm, bias_ref),
+        (gain_hbm, gain_ref),
+    )
+    l_scalars = [load(src, dst, 9 + k) for k, (src, dst) in enumerate(scalars)]
+    l_p = load(pf_hbm, pf_v, 5)
+    l_s = load(st_hbm, st_v, 6)
     l_r = load(wr_hbm, wr_v, 2)
     l_v = load(wv_hbm, wv_v, 3)
     l_g = load(wg_hbm, wg_v, 4)
-    l_p = load(pf_hbm, pf_v, 5)
-    l_s0 = load(st_hbm.at[pl.ds(0, 16)], st_v.at[pl.ds(0, 16)], 6)
-    l_s1 = load(st_hbm.at[pl.ds(16, 16)], st_v.at[pl.ds(16, 16)], 7)
     l_o = load(wo_hbm, wo_v, 8)
+
+    barrier = pltpu.get_barrier_semaphore()
+    greeted = 0
+    for i in range(N_DP):
+        for j in range(N_X):
+            if i or j:
+                to = ((me_d + i) % N_DP, vid((x + j) % N_X, c))
+                pl.semaphore_signal(barrier, inc=1, device_id=to, device_id_type=MESH)
+                greeted += 1
+    for j in range(N_X):
+        to = (me_d, vid((x + j) % N_X, 1 - c))
+        pl.semaphore_signal(barrier, inc=1, device_id=to, device_id_type=MESH)
+        greeted += 1
+
+    l_x.wait()
+    l_qk.wait()
     xin = x_v[...].reshape(STEPS * ROWS, WIDTH)
     joined = dot(xin, wqk_v[...]).astype(BF16)
     joined_f = joined.astype(F32)
+    for copy in l_scalars:
+        copy.wait()
     pick = jnp.zeros((N_DP, ROWS), F32)
     for t in range(STEPS):
         for j in range(REPLACED):
-            hit = (iota((N_DP, ROWS), 0) == own_ref[t, me_d, j]) & (iota((N_DP, ROWS), 1) == fin_ref[t, me_d, j])
+            hit = (iota((N_DP, ROWS), 0) == own_ref[t, j, me_d]) & (iota((N_DP, ROWS), 1) == fin_ref[t, j, me_d])
             pick = jnp.where(hit, 1.0, pick)
     pick = pick.astype(BF16)
     for t in range(STEPS):
@@ -154,21 +179,59 @@
 
     for o in range(N_DP):
         snd_f[o] = block_of(ROWS + o)
-    pl.semaphore_wait(barrier, N_DP + N_VALUE - 2)
-
-    def foreign(i):
+    pl.semaphore_wait(barrier, greeted)
+
+    def foreign(i, j):
         dst = (me_d + i) % N_DP
         return pltpu.make_async_remote_copy(
             src_ref=snd_f.at[dst],
             dst_ref=gbuf.at[me_v, ROWS + me_d],
-            send_sem=fs.at[i],
-            recv_sem=fr.at[i],
-            device_id=(dst, me_v),
+            send_sem=fs.at[j],
+            recv_sem=fr.at[j],
+            device_id=(dst, vid((x + j) % N_X, c)),
             device_id_type=MESH,
         )
 
-    for i in range(1, N_DP):
-        foreign(i).start()
+    def foreign_all(j):
+        slot = vid((x + N_X - j) % N_X, c)
+        first = 1 if j == 0 else 0
+        rows = pl.ds(ROWS, N_DP - first)
+        return pltpu.make_async_remote_copy(
+            src_ref=gbuf.at[slot, rows],
+            dst_ref=gbuf.at[slot, rows],
+            send_sem=fs.at[j],
+            recv_sem=fr.at[j],
+            device_id=(me_d, partner),
+            device_id_type=MESH,
+        )
+
+    def foreign_forward(j):
+        slot = vid((x + N_X - j) % N_X, c)
+        rows = pl.ds(ROWS, N_DP)
+        return pltpu.make_async_remote_copy(
+            src_ref=gbuf.at[slot, rows],
+            dst_ref=gbuf.at[slot, rows],
+            send_sem=fps.at[j],
+            recv_sem=fpr.at[j],
+            device_id=(me_d, partner),
+            device_id_type=MESH,
+        )
+
+    def foreign_forwarded(j):
+        slot = vid((x + N_X - j) % N_X, 1 - c)
+        rows = pl.ds(ROWS, N_DP)
+        pltpu.make_async_remote_copy(
+            src_ref=gbuf.at[slot, rows],
+            dst_ref=gbuf.at[slot, rows],
+            send_sem=fps.at[j],
+            recv_sem=fpr.at[j],
+            device_id=(me_d, partner),
+            device_id_type=MESH,
+        ).wait_recv()
+
+    for j in (2, 1, 3, 0):
+        for i in range(1 if j == 0 else 0, N_DP):
+            foreign(i, j).start()
     gbuf[me_v, ROWS + me_d] = snd_f[me_d]
     for r in range(CHUNK):
         gbuf[me_v, r] = block_of(r)
@@ -237,19 +300,20 @@
     send_own(FIRST)
     for r in range(CHUNK, 2 * CHUNK):
         gbuf[me_v, r] = block_of(r)
+    send_own(LAST)
     l_r.wait()
-    rates = dot(xin, wr_v[...])
-    for i in range(1, N_DP):
-        foreign(i).wait_recv()
-    send_own(FOREIGN)
-    send_own(LAST)
+    rates = dot_t(xin, wr_v[...])
     l_v.wait()
     val_s[...] = dot(xin, wv_v[...])
     forward_near(FIRST)
     l_g.wait()
     gate_s[...] = dot(xin, wg_v[...])
+    forward_near(LAST)
     forward_far(FIRST)
-    forward_near(FOREIGN)
+    for j in (0, 1, 3, 2):
+        foreign_all(j).wait_recv()
+        foreign_forward(j).start()
+    forward_far(LAST)
 
     lane = iota((8, 128), 1)
     sub = iota((8, 128), 0)
@@ -291,7 +355,7 @@
             slot = jnp.int32(0)
             for t in range(STEPS):
                 for j in range(REPLACED):
-                    slot = jnp.where(own_ref[t, d, j] == me_d, slot_ref[t, d, j], slot)
+                    slot = jnp.where(own_ref[t, j, d] == me_d, slot_ref[t, j, d], slot)
             qk = gbuf[:, ROWS + d].reshape(N_VALUE * TILE, DK)
             blocks = contract(qk, pf_v[slot])
             rsnd[d] = jnp.concatenate(blocks, axis=0).astype(BF16)
@@ -314,20 +378,17 @@
             device_id_type=MESH,
         )
 
-    all_here(FIRST)
-    l_s0.wait()
-    own_rows(0, CHUNK)
-    forward_far(FOREIGN)
-    forward_near(LAST)
-    all_here(FOREIGN)
     l_p.wait()
+    for j in (0, 1, 3, 2):
+        foreign_forwarded(j)
     foreign_rows()
     for i in range(1, N_DP):
         back(i).start()
     rrcv[me_d] = rsnd[me_d]
-    forward_far(LAST)
+    l_s.wait()
+    all_here(FIRST)
+    own_rows(0, CHUNK)
     all_here(LAST)
-    l_s1.wait()
     own_rows(CHUNK, CHUNK)
 
     gram = [msc[GROUPS, pl.ds(k, ROWS, stride=8), :] for k in range(2 * STEPS)]
@@ -370,7 +431,7 @@
     for t in range(STEPS):
         hit = jnp.zeros((ROWS, 128), jnp.bool_)
         for j in range(REPLACED):
-            done, owner = fin_ref[t, me_d, j], own_ref[t, me_d, j]
+            done, owner = fin_ref[t, j, me_d], own_ref[t, j, me_d]
             hit = hit | (row == done)
             latest = jnp.where(row_o == done, owner, latest)
             owner_of = jnp.where(row == done, owner, owner_of)
@@ -507,10 +568,12 @@
         total = total + r2_rcv[k].astype(F32)
     out_ref[...] = total.astype(BF16)
 
+    for j in range(N_X):
+        foreign_all(j).wait_send()
+        foreign_forward(j).wait_send()
     for i in range(1, N_DP):
-        foreign(i).wait_send()
         back(i).wait_send()
-    for chunk in range(3):
+    for chunk in range(2):
         for k in range(9):
             hop(chunk, k).wait_send()
     for i in range(1, N_VALUE):
@@ -537,20 +600,25 @@
     new_owner,
     new_slot,
 ):
-    smem = pl.BlockSpec(memory_space=pltpu.SMEM)
     hbm = pl.BlockSpec(memory_space=pl.ANY)
     dma = pltpu.SemaphoreType.DMA
     produced = pl.pallas_call(
         kernel,
         out_shape=jax.ShapeDtypeStruct((STEPS * ROWS, PIECE), BF16),
-        in_specs=[smem] * 6 + [hbm] * 8,
+        in_specs=[hbm] * 14,
         out_specs=pl.BlockSpec(memory_space=pltpu.VMEM),
         scratch_shapes=[
+            pltpu.SMEM((STEPS, REPLACED, N_DP), jnp.int32),
+            pltpu.SMEM((STEPS, REPLACED, N_DP), jnp.int32),
+            pltpu.SMEM((STEPS, REPLACED, N_DP), jnp.int32),
+            pltpu.SMEM((H,), F32),
+            pltpu.SMEM((H,), F32),
+            pltpu.SMEM((DV // N_VALUE,), F32),
             pltpu.VMEM((STEPS, ROWS, WIDTH), BF16),
             pltpu.VMEM((WIDTH, COLS), BF16),
             pltpu.VMEM((WIDTH, COLS), BF16),
             pltpu.VMEM((WIDTH, COLS), BF16),
-            pltpu.VMEM((WIDTH, 2 * H), BF16),
+            pltpu.VMEM((2 * H, WIDTH), BF16),
             pltpu.VMEM((COLS, WIDTH), BF16),
             pltpu.VMEM((ROWS, 16, H, DK), F32),
             pltpu.VMEM((16, 16, H, DK), F32),
@@ -570,11 +638,13 @@
             pltpu.VMEM((N_X, STEPS * ROWS, PIECE), F32),
             pltpu.VMEM((N_X - 1, STEPS * ROWS, PIECE), BF16),
             pltpu.VMEM((N_X - 1, STEPS * ROWS, PIECE), BF16),
-            dma((9,)),
-            dma((3, 9)),
-            dma((3, 9)),
-            dma((N_DP,)),
-            dma((N_DP,)),
+            dma((15,)),
+            dma((2, 9)),
+            dma((2, 9)),
+            dma((N_X,)),
+            dma((N_X,)),
+            dma((N_X,)),
+            dma((N_X,)),
             dma((N_DP,)),
             dma((N_DP,)),
             dma((N_VALUE,)),
@@ -589,9 +659,9 @@
         ),
         name="delta_steps",
     )(
-        finished,
-        new_owner,
-        new_slot,
+        finished.transpose(0, 2, 1),
+        new_owner.transpose(0, 2, 1),
+        new_slot.transpose(0, 2, 1),
         log_decay,
         decay_bias,
         norm_gain,
@@ -599,7 +669,7 @@
         qk_weight,
         value_weight,
         output_gate_weight,
-        rate_weight,
+        rate_weight.T,
         out_weight,
         states,
         prefilled,

time: 53 us -> 43.1 us (0.81)
  local copies, waits for them, and re-layouts: 7.58 us -> 1.47 us
  Pallas kernels: 45 us -> 41.5 us
    unnamed x5 -> x1, local copies, waits for them, and re-layouts: 7.58 us -> 1.47 us
    pallas_call x1, Pallas kernels: 45 us -> 41.5 us  [on_device(): pl.pallas_call(kernel, out_shape=jax.ShapeDtypeStruct((STEPS * ROWS, PIEC...]
where the time goes in v2:
time: 43.1 us; the launch traced here: 42.9 us
  Pallas kernels  41.5 us (96%)
  local copies, waits for them, and re-layouts  1.47 us (3%)
    pallas_call x1, Pallas kernels, on_device(): pl.pallas_call(kernel, out_shape=jax.ShapeDtypeStruct((STEPS * ROWS, PIEC...  41.5 us
    unnamed x1, local copies, waits for them, and re-layouts  1.47 us

profile of v2, /device:TPU:1, one launch (start us, length us, event | category | flops | bytes accessed | tf_op | source)
XLA Modules:
  0.0 42.9 jit_solution(17232948006068068471)
XLA Ops:
  0.0 41.5 %delta_steps.1 = bf16[128,256]{1,0:T(8,128)(2,1)} custom-call(s32[4,2,16]{2,1,0:T(2,128)} %bitcast.7, s32[4,2,16]{2,1,0:T(2,128)} %bitcast.8, s32[4,2,16]{2,1,0:T(2,128)} %bitcast.9, f32[32]{0:T(128)} %logd_hbm.1, f32[32]{0:T(128)} %bias_hbm.1, f32[16]{0:T(128)} %gain_hbm.1, bf16[4,32,2048]{2,1,0:T(8,128)(2,1)} %x_hbm.1, bf16[2048,512]{1,0:T(8,128)(2,1)} %wqk_hbm.1, ...), custom_call_target="tpu_custom_call" | custom-call | tf_op jit(solution)/shard_map/delta_steps/pallas_call | solution.py:605
  41.5 1.5 %copy.16 = bf16[4,32,256]{2,1,0:T(8,128)(2,1)} copy(bf16[4,32,256]{2,1,0:T(8,128)(2,1)} %bitcast.6) | data formatting | bytes 131072

commit v3 on v2

--- a/solution.py
+++ b/solution.py
@@ -27,10 +27,27 @@
 HEADS = 4
 TILE = HEADS * STEPS
 GROUPS = COLS // 128
+ALL = STEPS * ROWS
+
+PAIRS = [(s, t) for t in range(STEPS) for s in range(t + 1)]
+VALUES, GATING = 0, GROUPS * ALL
+RETAIN = 2 * GROUPS * ALL
+STRENGTH, INV_K, INV_Q = RETAIN + ALL, RETAIN + 2 * ALL, RETAIN + 3 * ALL
+KEY_KEY = RETAIN + 4 * ALL
+KEY_QUERY = KEY_KEY + len(PAIRS) * ROWS
+QUANTITIES = KEY_QUERY // ROWS + len(PAIRS)
 
 FIRST, LAST = 0, 1
 BASE = (0, 16)
 CHUNK = 16
+
+
+def ring(k):
+    return min(k, N_X - k)
+
+
+PLANE = sorted(((a, b) for a in range(N_X) for b in range(N_X)), key=lambda o: -ring(o[0]) - ring(o[1]))
+SPACE = sorted(((i, j) for i in range(N_DP) for j in range(N_X)), key=lambda o: -sum(map(ring, (*PLANE[o[0]], o[1]))))
 
 
 def iota(shape, dim):
@@ -82,15 +99,18 @@
     rsnd,
     rrcv,
     rf,
-    val_s,
-    gate_s,
+    rowq,
+    slotq,
     gat_s,
     sqbuf,
+    ssqbuf,
     r1_snd,
     r1_rcv,
     part,
     r2_snd,
     r2_rcv,
+    s_snd,
+    s_rcv,
     loc,
     ag_s,
     ag_r,
@@ -106,6 +126,10 @@
     r1r,
     r2s,
     r2r,
+    sqs,
+    sqr,
+    ss,
+    sr,
 ):
     me_d = lax.axis_index("dp")
     me_v = lax.axis_index("value")
@@ -117,6 +141,22 @@
         return xx * 2 + cc
 
     right, left, partner = vid(xr, c), vid(xl, c), vid(x, 1 - c)
+
+    def peer(i):
+        dz, dy = PLANE[i]
+        return ((me_d // N_X + dz) % N_X) * N_X + (me_d % N_X + dy) % N_X
+
+    barrier = pltpu.get_barrier_semaphore()
+    greeted = 0
+    for i, j in SPACE:
+        if PLANE[i] != (0, 0) or j:
+            to = (peer(i), vid((x + j) % N_X, c))
+            pl.semaphore_signal(barrier, inc=1, device_id=to, device_id_type=MESH)
+            greeted += 1
+    for j in range(N_X):
+        to = (me_d, vid((x + j) % N_X, 1 - c))
+        pl.semaphore_signal(barrier, inc=1, device_id=to, device_id_type=MESH)
+        greeted += 1
 
     def load(src, dst, k):
         cp = pltpu.make_async_copy(src, dst, loc.at[k])
@@ -134,25 +174,12 @@
         (gain_hbm, gain_ref),
     )
     l_scalars = [load(src, dst, 9 + k) for k, (src, dst) in enumerate(scalars)]
-    l_p = load(pf_hbm, pf_v, 5)
-    l_s = load(st_hbm, st_v, 6)
     l_r = load(wr_hbm, wr_v, 2)
     l_v = load(wv_hbm, wv_v, 3)
     l_g = load(wg_hbm, wg_v, 4)
+    l_p = load(pf_hbm, pf_v, 5)
+    l_s = load(st_hbm, st_v, 6)
     l_o = load(wo_hbm, wo_v, 8)
-
-    barrier = pltpu.get_barrier_semaphore()
-    greeted = 0
-    for i in range(N_DP):
-        for j in range(N_X):
-            if i or j:
-                to = ((me_d + i) % N_DP, vid((x + j) % N_X, c))
-                pl.semaphore_signal(barrier, inc=1, device_id=to, device_id_type=MESH)
-                greeted += 1
-    for j in range(N_X):
-        to = (me_d, vid((x + j) % N_X, 1 - c))
-        pl.semaphore_signal(barrier, inc=1, device_id=to, device_id_type=MESH)
-        greeted += 1
 
     l_x.wait()
     l_qk.wait()
@@ -182,7 +209,7 @@
     pl.semaphore_wait(barrier, greeted)
 
     def foreign(i, j):
-        dst = (me_d + i) % N_DP
+        dst = peer(i)
         return pltpu.make_async_remote_copy(
             src_ref=snd_f.at[dst],
             dst_ref=gbuf.at[me_v, ROWS + me_d],
@@ -229,8 +256,8 @@
             device_id_type=MESH,
         ).wait_recv()
 
-    for j in (2, 1, 3, 0):
-        for i in range(1 if j == 0 else 0, N_DP):
+    for i, j in SPACE:
+        if PLANE[i] != (0, 0) or j:
             foreign(i, j).start()
     gbuf[me_v, ROWS + me_d] = snd_f[me_d]
     for r in range(CHUNK):
@@ -301,13 +328,30 @@
     for r in range(CHUNK, 2 * CHUNK):
         gbuf[me_v, r] = block_of(r)
     send_own(LAST)
+
+    seg = iota((1, 128), 1) // H
+    in_seg = iota((1, 128), 1) % H
     l_r.wait()
     rates = dot_t(xin, wr_v[...])
+    decay = jnp.zeros((1, 128), F32)
+    bias = jnp.zeros((1, 128), F32)
+    for h in range(H):
+        decay = jnp.where(in_seg == h, logd_ref[h], decay)
+        bias = jnp.where(in_seg == h, bias_ref[h], bias)
+    wide = jnp.concatenate([rates, rates], axis=1)
+    turned = pltpu.roll(wide, H, 1)
+    odd = seg % 2 == 1
+    rowq[RETAIN : RETAIN + ALL] = jnp.exp(-jnp.exp(decay) * jax.nn.softplus(jnp.where(odd, wide, turned) + bias))
+    rowq[STRENGTH : STRENGTH + ALL] = jax.nn.sigmoid(jnp.where(odd, turned, wide))
     l_v.wait()
-    val_s[...] = dot(xin, wv_v[...])
+    values = dot(xin, wv_v[...])
+    for g in range(GROUPS):
+        rowq[VALUES + g * ALL : VALUES + (g + 1) * ALL] = values[:, g * 128 : (g + 1) * 128]
     forward_near(FIRST)
     l_g.wait()
-    gate_s[...] = dot(xin, wg_v[...])
+    gating = dot(xin, wg_v[...])
+    for g in range(GROUPS):
+        rowq[GATING + g * ALL : GATING + (g + 1) * ALL] = gating[:, g * 128 : (g + 1) * 128]
     forward_near(LAST)
     forward_far(FIRST)
     for j in (0, 1, 3, 2):
@@ -368,7 +412,7 @@
         lax.fori_loop(0, N_DP // 2, two, 0)
 
     def back(i):
-        dst = (me_d + i) % N_DP
+        dst = peer(i)
         return pltpu.make_async_remote_copy(
             src_ref=rsnd.at[dst],
             dst_ref=rrcv.at[me_d],
@@ -382,8 +426,9 @@
     for j in (0, 1, 3, 2):
         foreign_forwarded(j)
     foreign_rows()
-    for i in range(1, N_DP):
-        back(i).start()
+    for i in range(N_DP):
+        if PLANE[i] != (0, 0):
+            back(i).start()
     rrcv[me_d] = rsnd[me_d]
     l_s.wait()
     all_here(FIRST)
@@ -403,126 +448,134 @@
         qq = dot(gram[t], (src == head * 4 + t).astype(F32), **exact)
         inv_k.append(lax.rsqrt(kk + 1e-06))
         inv_q.append(lax.rsqrt(qq + 1e-06) * DK ** (-0.5))
-
-    def key_key(s, t):
-        return by_key[(STEPS + t) * ROWS : (STEPS + t + 1) * ROWS, s * 128 : (s + 1) * 128] * (inv_k[s] * inv_k[t])
-
-    def key_query(s, t):
-        return by_key[t * ROWS : (t + 1) * ROWS, s * 128 : (s + 1) * 128] * (inv_k[s] * inv_q[t])
-
-    seg = iota((1, 128), 1) // H
-    in_seg = iota((1, 128), 1) % H
-    decay = jnp.zeros((1, 128), F32)
-    bias = jnp.zeros((1, 128), F32)
-    for h in range(H):
-        decay = jnp.where(in_seg == h, logd_ref[h], decay)
-        bias = jnp.where(in_seg == h, bias_ref[h], bias)
-    wide = jnp.concatenate([rates, rates], axis=1)
-    turned = pltpu.roll(wide, H, 1)
-    odd = seg % 2 == 1
-    strength = jax.nn.sigmoid(jnp.where(odd, turned, wide))
-    retain = jnp.exp(-jnp.exp(decay) * jax.nn.softplus(jnp.where(odd, wide, turned) + bias))
-
-    row = iota((ROWS, 128), 0)
-    row_o = iota((ROWS, N_DP), 0)
-    latest = jnp.full((ROWS, N_DP), -1, jnp.int32)
-    owner_of = jnp.full((ROWS, 128), -1, jnp.int32)
-    fresh, replaced, takes = [], [], []
+        rowq[INV_K + t * ROWS : INV_K + (t + 1) * ROWS] = inv_k[t]
+        rowq[INV_Q + t * ROWS : INV_Q + (t + 1) * ROWS] = inv_q[t]
     for t in range(STEPS):
-        hit = jnp.zeros((ROWS, 128), jnp.bool_)
-        for j in range(REPLACED):
-            done, owner = fin_ref[t, j, me_d], own_ref[t, j, me_d]
-            hit = hit | (row == done)
-            latest = jnp.where(row_o == done, owner, latest)
-            owner_of = jnp.where(row == done, owner, owner_of)
-        fresh.append(hit)
-        replaced.append(owner_of >= 0)
-        takes.append((latest == iota((ROWS, N_DP), 1)).astype(BF16))
-
-    for i in range(1, N_DP):
-        back(i).wait_recv()
-    rf[...] = rrcv[...].astype(F32).reshape(N_DP * GROUPS * 8, 128)
-    returned = []
-    for k in range(2 * STEPS):
-        parts = [rf[pl.ds(g * 8 + k, N_DP, stride=GROUPS * 8), :] for g in range(GROUPS)]
-        returned.append(dot(takes[k % STEPS], jnp.concatenate(parts, axis=1).astype(BF16)))
-
-    readouts = [[None] * GROUPS for _ in range(STEPS)]
-    squares = [None] * STEPS
-    kks = {(s, t): key_key(s, t) for t in range(STEPS) for s in range(t)}
-    kqs = {(s, t): key_query(s, t) for t in range(STEPS) for s in range(t + 1)}
-    for g in range(GROUPS):
-        lanes = slice(g * 128, (g + 1) * 128)
-        written = []
-        kept = None
+        for s in range(t + 1):
+            if s < t:
+                at = KEY_KEY + PAIRS.index((s, t)) * ROWS
+                kk = by_key[(STEPS + t) * ROWS : (STEPS + t + 1) * ROWS, s * 128 : (s + 1) * 128]
+                rowq[at : at + ROWS] = kk * (inv_k[s] * inv_k[t])
+            at = KEY_QUERY + PAIRS.index((s, t)) * ROWS
+            kq = by_key[t * ROWS : (t + 1) * ROWS, s * 128 : (s + 1) * 128]
+            rowq[at : at + ROWS] = kq * (inv_k[s] * inv_q[t])
+
+    def recurrence(get, contracted, fresh):
+        readouts = [[None] * GROUPS for _ in range(STEPS)]
+        squares = [None] * STEPS
+        for g in range(GROUPS):
+            written = []
+            kept = None
+            for t in range(STEPS):
+                a, b = get(RETAIN + t * ROWS), get(STRENGTH + t * ROWS)
+                kept = a if kept is None else kept * a
+                written = [w * a for w in written]
+                if fresh is not None:
+                    kept = jnp.where(fresh[t], a, kept)
+                    written = [jnp.where(fresh[t], 0.0, w) for w in written]
+                memory = kept * contracted(g, STEPS + t) * get(INV_K + t * ROWS)
+                readout = kept * contracted(g, t) * get(INV_Q + t * ROWS)
+                for s, w in enumerate(written):
+                    at = PAIRS.index((s, t)) * ROWS
+                    memory = memory + w * get(KEY_KEY + at)
+                    readout = readout + w * get(KEY_QUERY + at)
+                update = (get(VALUES + g * ALL + t * ROWS) - memory) * b
+                readout = readout + update * get(KEY_QUERY + PAIRS.index((t, t)) * ROWS)
+                written.append(update)
+                readouts[t][g] = readout
+                square = readout * readout
+                squares[t] = square if g == 0 else squares[t] + square
+        packed = jnp.zeros_like(squares[0])
         for t in range(STEPS):
-            rows = slice(t * ROWS, (t + 1) * ROWS)
-            a, b = retain[rows], strength[rows]
-            kept = a if kept is None else jnp.where(fresh[t], a, kept * a)
-            written = [jnp.where(fresh[t], 0.0, w * a) for w in written]
-
-            def base(k):
-                mine = msc[g, pl.ds(k, ROWS, stride=8), :]
-                return jnp.where(replaced[t], returned[k][:, lanes], mine)
-
-            memory = kept * base(STEPS + t) * inv_k[t]
-            readout = kept * base(t) * inv_q[t]
-            for s, w in enumerate(written):
-                memory = memory + w * kks[s, t]
-                readout = readout + w * kqs[s, t]
-            update = (val_s[rows, lanes] - memory) * b
-            readout = readout + update * kqs[t, t]
-            written.append(update)
-            readouts[t][g] = readout
-            square = readout * readout
-            squares[t] = square if g == 0 else squares[t] + square
-    packed = jnp.zeros((ROWS, 128), F32)
+            total = squares[t] + pltpu.roll(squares[t], 64, 1)
+            total = total + pltpu.roll(total, 32, 1)
+            packed = jnp.where(seg == t, total, packed)
+        return readouts, packed
+
+    def silu_gain(readouts, get):
+        for g in range(GROUPS):
+            gain = jnp.zeros((1, 128), F32)
+            for e in range(4):
+                gain = jnp.where(seg == e, gain_ref[g * 4 + e], gain)
+            for t in range(STEPS):
+                gate = get(GATING + g * ALL + t * ROWS)
+                readouts[t][g] = readouts[t][g] * gain * (gate * jax.nn.sigmoid(gate))
+
+    def scalings(summed):
+        out = []
+        for t in range(STEPS):
+            total = jnp.where(seg == t, summed, 0.0)
+            total = total + pltpu.roll(total, 64, 1)
+            total = total + pltpu.roll(total, 32, 1)
+            out.append(lax.rsqrt(total * (1.0 / DV) + 1e-06))
+        return out
+
+    def exchange(buf, s_sem, r_sem):
+        def one(i, slot):
+            return pltpu.make_async_remote_copy(
+                src_ref=buf.at[slot],
+                dst_ref=buf.at[slot],
+                send_sem=s_sem.at[i],
+                recv_sem=r_sem.at[i],
+                device_id=(me_d, (me_v + i) % N_VALUE),
+                device_id_type=MESH,
+            )
+
+        sends = [one(i, me_v) for i in range(1, N_VALUE)]
+        arrivals = [one(i, (me_v + N_VALUE - i) % N_VALUE) for i in range(1, N_VALUE)]
+        return sends, arrivals
+
+    def row_get(at):
+        return rowq[at : at + ROWS]
+
+    readouts, packed = recurrence(row_get, lambda g, k: msc[g, pl.ds(k, ROWS, stride=8), :], None)
+    sqbuf[me_v] = packed.astype(BF16)
+    sq_sends, sq_arrivals = exchange(sqbuf, qs, qr)
+    for copy in sq_sends:
+        copy.start()
+
+    slots = [(t, j) for t in range(STEPS) for j in range(REPLACED)]
+    for k, (t, j) in enumerate(slots):
+        slotq[k * QUANTITIES : (k + 1) * QUANTITIES] = rowq[pl.ds(fin_ref[t, j, me_d], QUANTITIES, stride=ROWS), :]
+
+    def slot_get(at):
+        return slotq[pl.ds(at // ROWS, len(slots), stride=QUANTITIES), :]
+
+    silu_gain(readouts, row_get)
+    slot_of = jnp.full((ALL, 128), -1, jnp.int32)
+    take_of = jnp.full((ALL, len(slots) * STEPS), -1, jnp.int32)
+    for k, (t, j) in enumerate(slots):
+        done = fin_ref[t, j, me_d]
+        wide_row, thin_row = iota(slot_of.shape, 0), iota(take_of.shape, 0)
+        slot_of = jnp.where((wide_row % ROWS == done) & (wide_row // ROWS >= t), k, slot_of)
+        take_of = jnp.where((thin_row % ROWS == done) & (thin_row // ROWS >= t), k, take_of)
+    column = iota(take_of.shape, 1)
+    same_step = column // len(slots) == iota(take_of.shape, 0) // ROWS
+    take = ((take_of == column % len(slots)) & same_step).astype(BF16)
+
+    for i in range(N_DP):
+        if PLANE[i] != (0, 0):
+            back(i).wait_recv()
+    for k, (t, j) in enumerate(slots):
+        rf[k * GROUPS * 8 : (k + 1) * GROUPS * 8] = rrcv[own_ref[t, j, me_d]].astype(F32)
+    slot_row = iota((len(slots), 128), 0)
+    slot_readouts, slot_packed = recurrence(
+        slot_get,
+        lambda g, k: rf[pl.ds(g * 8 + k, len(slots), stride=GROUPS * 8), :],
+        [slot_row // REPLACED == t for t in range(STEPS)],
+    )
+    ssqbuf[me_v] = slot_packed
+    ssq_sends, ssq_arrivals = exchange(ssqbuf, sqs, sqr)
+    for copy in ssq_sends:
+        copy.start()
+    silu_gain(slot_readouts, slot_get)
+
+    for copy in sq_arrivals:
+        copy.wait_recv()
+    scales = scalings(jnp.sum(sqbuf[...].astype(F32), axis=0))
     for t in range(STEPS):
-        total = squares[t] + pltpu.roll(squares[t], 64, 1)
-        total = total + pltpu.roll(total, 32, 1)
-        packed = jnp.where(seg == t, total, packed)
-    sqbuf[me_v] = packed.astype(BF16)
-
-    def square_copy(i):
-        return pltpu.make_async_remote_copy(
-            src_ref=sqbuf.at[me_v],
-            dst_ref=sqbuf.at[me_v],
-            send_sem=qs.at[i],
-            recv_sem=qr.at[i],
-            device_id=(me_d, (me_v + i) % N_VALUE),
-            device_id_type=MESH,
-        )
-
-    def square_here(i):
-        origin = (me_v + N_VALUE - i) % N_VALUE
-        pltpu.make_async_remote_copy(
-            src_ref=sqbuf.at[origin],
-            dst_ref=sqbuf.at[origin],
-            send_sem=qs.at[i],
-            recv_sem=qr.at[i],
-            device_id=(me_d, (me_v + i) % N_VALUE),
-            device_id_type=MESH,
-        ).wait_recv()
-
-    for i in range(1, N_VALUE):
-        square_copy(i).start()
-    for g in range(GROUPS):
-        gain = jnp.zeros((1, 128), F32)
-        for e in range(4):
-            gain = jnp.where(seg == e, gain_ref[g * 4 + e], gain)
-        for t in range(STEPS):
-            gating = gate_s[t * ROWS : (t + 1) * ROWS, g * 128 : (g + 1) * 128]
-            readouts[t][g] = readouts[t][g] * gain * (gating * jax.nn.sigmoid(gating))
-    for i in range(1, N_VALUE):
-        square_here(i)
-    summed = jnp.sum(sqbuf[...].astype(F32), axis=0)
-    for t in range(STEPS):
-        total = jnp.where(seg == t, summed, 0.0)
-        total = total + pltpu.roll(total, 64, 1)
-        total = total + pltpu.roll(total, 32, 1)
-        scaling = lax.rsqrt(total * (1.0 / DV) + 1e-06)
         for g in range(GROUPS):
-            gat_s[t * ROWS : (t + 1) * ROWS, g * 128 : (g + 1) * 128] = (readouts[t][g] * scaling).astype(BF16)
+            gat_s[t * ROWS : (t + 1) * ROWS, g * 128 : (g + 1) * 128] = (readouts[t][g] * scales[t]).astype(BF16)
 
     l_o.wait()
     gated = gat_s[...]
@@ -561,27 +614,67 @@
         first_copy(k).wait_recv()
         r2_snd[k] = (part[k] + r1_rcv[k].astype(F32)).astype(BF16)
         second_copy(k).start()
+
+    for copy in ssq_arrivals:
+        copy.wait_recv()
+    slot_scales = scalings(jnp.sum(ssqbuf[...], axis=0))
+    slot_gated = jnp.concatenate(
+        [
+            jnp.concatenate([slot_readouts[t][g] * slot_scales[t] for g in range(GROUPS)], axis=1)
+            for t in range(STEPS)
+        ],
+        axis=0,
+    ).astype(BF16)
+
+    def slot_project(to):
+        at = pl.multiple_of(to * PIECE, PIECE)
+        return dot(slot_gated, wo_v[:, pl.ds(at, PIECE)])
+
+    def slot_copy(i):
+        return pltpu.make_async_remote_copy(
+            src_ref=s_snd.at[i],
+            dst_ref=s_rcv.at[i],
+            send_sem=ss.at[i],
+            recv_sem=sr.at[i],
+            device_id=(me_d, (me_v + i) % N_VALUE),
+            device_id_type=MESH,
+        )
+
+    for i in (4, 3, 5, 2, 6, 1, 7):
+        s_snd[i] = slot_project((me_v + i) % N_VALUE).astype(BF16)
+        slot_copy(i).start()
+    slot_total = slot_project(me_v)
+
     first_copy(3).wait_recv()
     total = part[3] + r1_rcv[3].astype(F32)
     for k in (1, 2, 0):
         second_copy(k).wait_recv()
         total = total + r2_rcv[k].astype(F32)
-    out_ref[...] = total.astype(BF16)
+    for i in (1, 7, 2, 6, 3, 5, 4):
+        slot_copy(i).wait_recv()
+        slot_total = slot_total + s_rcv[i].astype(F32)
+    chosen = dot(take, slot_total.astype(BF16))
+    for half in range(PIECE // 128):
+        lanes = slice(half * 128, (half + 1) * 128)
+        out_ref[:, lanes] = jnp.where(slot_of >= 0, chosen[:, lanes], total[:, lanes]).astype(BF16)
 
     for j in range(N_X):
         foreign_all(j).wait_send()
         foreign_forward(j).wait_send()
-    for i in range(1, N_DP):
-        back(i).wait_send()
+    for i in range(N_DP):
+        if PLANE[i] != (0, 0):
+            back(i).wait_send()
     for chunk in range(2):
         for k in range(9):
             hop(chunk, k).wait_send()
-    for i in range(1, N_VALUE):
-        square_copy(i).wait_send()
+    for copy in sq_sends + ssq_sends:
+        copy.wait_send()
     for k in range(N_X):
         first_copy(k).wait_send()
     for k in range(N_X - 1):
         second_copy(k).wait_send()
+    for i in range(1, N_VALUE):
+        slot_copy(i).wait_send()
 
 
 def on_device(
@@ -628,16 +721,19 @@
             pltpu.VMEM((GROUPS + 1, ROWS * 8, 128), F32),
             pltpu.VMEM((N_DP, GROUPS * 8, 128), BF16),
             pltpu.VMEM((N_DP, GROUPS * 8, 128), BF16),
-            pltpu.VMEM((N_DP * GROUPS * 8, 128), F32),
-            pltpu.VMEM((STEPS * ROWS, COLS), F32),
-            pltpu.VMEM((STEPS * ROWS, COLS), F32),
+            pltpu.VMEM((STEPS * REPLACED * GROUPS * 8, 128), F32),
+            pltpu.VMEM((QUANTITIES * ROWS, 128), F32),
+            pltpu.VMEM((STEPS * REPLACED * QUANTITIES, 128), F32),
             pltpu.VMEM((STEPS * ROWS, COLS), BF16),
             pltpu.VMEM((N_VALUE, ROWS, 128), BF16),
+            pltpu.VMEM((N_VALUE, STEPS * REPLACED, 128), F32),
             pltpu.VMEM((N_X, STEPS * ROWS, PIECE), BF16),
             pltpu.VMEM((N_X, STEPS * ROWS, PIECE), BF16),
             pltpu.VMEM((N_X, STEPS * ROWS, PIECE), F32),
             pltpu.VMEM((N_X - 1, STEPS * ROWS, PIECE), BF16),
             pltpu.VMEM((N_X - 1, STEPS * ROWS, PIECE), BF16),
+            pltpu.VMEM((N_VALUE, STEPS * STEPS * REPLACED, PIECE), BF16),
+            pltpu.VMEM((N_VALUE, STEPS * STEPS * REPLACED, PIECE), BF16),
             dma((15,)),
             dma((2, 9)),
             dma((2, 9)),
@@ -653,6 +749,10 @@
             dma((N_X,)),
             dma((N_X - 1,)),
             dma((N_X - 1,)),
+            dma((N_VALUE,)),
+            dma((N_VALUE,)),
+            dma((N_VALUE,)),
+            dma((N_VALUE,)),
         ],
         compiler_params=pltpu.CompilerParams(
             collective_id=0, has_side_effects=True, vmem_limit_bytes=56 * 2**20

time: 43.1 us -> 44.1 us (1.023)
  Pallas kernels: 41.5 us -> 42.5 us
    pallas_call x1, Pallas kernels: 41.5 us -> 42.5 us  [on_device(): pl.pallas_call(kernel, out_shape=jax.ShapeDtypeStruct((STEPS * ROWS, PIEC...]
where the time goes in v3:
time: 44.1 us; the launch traced here: 44 us
  Pallas kernels  42.5 us (96%)
  local copies, waits for them, and re-layouts  1.47 us (3%)
    pallas_call x1, Pallas kernels, on_device(): pl.pallas_call(kernel, out_shape=jax.ShapeDtypeStruct((STEPS * ROWS, PIEC...  42.5 us
    unnamed x1, local copies, waits for them, and re-layouts  1.47 us

profile of v3, /device:TPU:1, one launch (start us, length us, event | category | flops | bytes accessed | tf_op | source)
XLA Modules:
  0.0 44.0 jit_solution(6023691255320977941)
XLA Ops:
  0.0 42.5 %delta_steps.1 = bf16[128,256]{1,0:T(8,128)(2,1)} custom-call(s32[4,2,16]{2,1,0:T(2,128)} %bitcast.7, s32[4,2,16]{2,1,0:T(2,128)} %bitcast.8, s32[4,2,16]{2,1,0:T(2,128)} %bitcast.9, f32[32]{0:T(128)} %logd_hbm.1, f32[32]{0:T(128)} %bias_hbm.1, f32[16]{0:T(128)} %gain_hbm.1, bf16[4,32,2048]{2,1,0:T(8,128)(2,1)} %x_hbm.1, bf16[2048,512]{1,0:T(8,128)(2,1)} %wqk_hbm.1, ...), custom_call_target="tpu_custom_call" | custom-call | tf_op jit(solution)/shard_map/delta_steps/pallas_call | solution.py:698
  42.5 1.5 %copy.16 = bf16[4,32,256]{2,1,0:T(8,128)(2,1)} copy(bf16[4,32,256]{2,1,0:T(8,128)(2,1)} %bitcast.6) | data formatting | bytes 131072

commit v4 on v3

--- a/solution.py
+++ b/solution.py
@@ -40,6 +40,7 @@
 FIRST, LAST = 0, 1
 BASE = (0, 16)
 CHUNK = 16
+UNROLL = 8
 
 
 def ring(k):
@@ -135,12 +136,11 @@
     me_v = lax.axis_index("value")
     x = me_v // 2
     c = me_v % 2
-    xr, xl, xo = (x + 1) % N_X, (x + 3) % N_X, (x + 2) % N_X
 
     def vid(xx, cc):
         return xx * 2 + cc
 
-    right, left, partner = vid(xr, c), vid(xl, c), vid(x, 1 - c)
+    partner = vid(x, 1 - c)
 
     def peer(i):
         dz, dy = PLANE[i]
@@ -263,22 +263,8 @@
     for r in range(CHUNK):
         gbuf[me_v, r] = block_of(r)
 
-    def hop(chunk, k):
-        slot, half, to = (
-            (me_v, None, right),
-            (me_v, None, left),
-            (me_v, None, partner),
-            (left, 0, right),
-            (right, 1, left),
-            (left, None, partner),
-            (right, None, partner),
-            (vid(xo, c), 0, partner),
-            (vid(xo, c), 1, partner),
-        )[k]
-        return ag_copy(chunk, k, slot, half, to)
-
-    def ag_copy(chunk, k, slot, half, to):
-        rows = pl.ds(BASE[chunk], CHUNK) if half is None else pl.ds(BASE[chunk] + half * 8, 8)
+    def gather(chunk, k, slot, to):
+        rows = pl.ds(BASE[chunk], CHUNK)
         return pltpu.make_async_remote_copy(
             src_ref=gbuf.at[slot, rows],
             dst_ref=gbuf.at[slot, rows],
@@ -288,41 +274,31 @@
             device_id_type=MESH,
         )
 
-    def arrived(chunk, k):
-        slot, half = (
-            (left, None),
-            (right, None),
-            (partner, None),
-            (vid(xo, c), 0),
-            (vid(xo, c), 1),
-            (vid(xl, 1 - c), None),
-            (vid(xr, 1 - c), None),
-            (vid(xo, 1 - c), 0),
-            (vid(xo, 1 - c), 1),
-        )[k]
-        ag_copy(chunk, k, slot, half, partner).wait_recv()
+    def along(chunk, j):
+        return gather(chunk, j, me_v, vid((x + j) % N_X, c) if j else partner)
+
+    def arrived(chunk, j):
+        gather(chunk, j, vid((x + N_X - j) % N_X, c) if j else partner, partner).wait_recv()
+
+    def forward(chunk, j):
+        return gather(chunk, N_X - 1 + j, vid((x + N_X - j) % N_X, c), partner)
+
+    def forwarded(chunk, j):
+        gather(chunk, N_X - 1 + j, vid((x + N_X - j) % N_X, 1 - c), partner).wait_recv()
 
     def send_own(chunk):
-        for k in range(3):
-            hop(chunk, k).start()
-
-    def forward_near(chunk):
+        for j in (2, 1, 3, 0):
+            along(chunk, j).start()
+
+    def pass_on(chunk):
+        for j in (1, 3, 2):
+            arrived(chunk, j)
+            forward(chunk, j).start()
+
+    def all_here(chunk):
         arrived(chunk, 0)
-        hop(chunk, 3).start()
-        hop(chunk, 5).start()
-        arrived(chunk, 1)
-        hop(chunk, 4).start()
-        hop(chunk, 6).start()
-
-    def forward_far(chunk):
-        arrived(chunk, 3)
-        hop(chunk, 7).start()
-        arrived(chunk, 4)
-        hop(chunk, 8).start()
-
-    def all_here(chunk):
-        for k in (2, 5, 6, 7, 8):
-            arrived(chunk, k)
+        for j in (1, 3, 2):
+            forwarded(chunk, j)
 
     send_own(FIRST)
     for r in range(CHUNK, 2 * CHUNK):
@@ -347,17 +323,14 @@
     values = dot(xin, wv_v[...])
     for g in range(GROUPS):
         rowq[VALUES + g * ALL : VALUES + (g + 1) * ALL] = values[:, g * 128 : (g + 1) * 128]
-    forward_near(FIRST)
     l_g.wait()
     gating = dot(xin, wg_v[...])
     for g in range(GROUPS):
         rowq[GATING + g * ALL : GATING + (g + 1) * ALL] = gating[:, g * 128 : (g + 1) * 128]
-    forward_near(LAST)
-    forward_far(FIRST)
     for j in (0, 1, 3, 2):
         foreign_all(j).wait_recv()
         foreign_forward(j).start()
-    forward_far(LAST)
+    pass_on(FIRST)
 
     lane = iota((8, 128), 1)
     sub = iota((8, 128), 0)
@@ -379,20 +352,19 @@
         return [diagonal(full[:, g * 128 : (g + 1) * 128], state_masks) for g in range(GROUPS)]
 
     def own_rows(first, count):
-        def one(r, _):
+        def one(r):
             qk = gbuf[:, r].reshape(N_VALUE * TILE, DK)
             at = pl.multiple_of(r * 8, 8)
             for g, block in enumerate(contract(qk, st_v[r])):
                 msc[g, pl.ds(at, 8)] = block
             msc[GROUPS, pl.ds(at, 8)] = diagonal(dot_t(qk, qk), gram_masks)
+
+        def some(i, _):
+            for k in range(UNROLL):
+                one(first + UNROLL * i + k)
             return 0
 
-        def two(i, _):
-            one(first + 2 * i, 0)
-            one(first + 2 * i + 1, 0)
-            return 0
-
-        lax.fori_loop(0, count // 2, two, 0)
+        lax.fori_loop(0, count // UNROLL, some, 0)
 
     def foreign_rows():
         def one(d):
@@ -404,12 +376,12 @@
             blocks = contract(qk, pf_v[slot])
             rsnd[d] = jnp.concatenate(blocks, axis=0).astype(BF16)
 
-        def two(i, _):
-            one(2 * i)
-            one(2 * i + 1)
+        def some(i, _):
+            for k in range(UNROLL):
+                one(UNROLL * i + k)
             return 0
 
-        lax.fori_loop(0, N_DP // 2, two, 0)
+        lax.fori_loop(0, N_DP // UNROLL, some, 0)
 
     def back(i):
         dst = peer(i)
@@ -430,6 +402,7 @@
         if PLANE[i] != (0, 0):
             back(i).start()
     rrcv[me_d] = rsnd[me_d]
+    pass_on(LAST)
     l_s.wait()
     all_here(FIRST)
     own_rows(0, CHUNK)
@@ -579,7 +552,7 @@
 
     l_o.wait()
     gated = gat_s[...]
-    order = (xo, xr, xl, x)
+    order = [(x + j) % N_X for j in (2, 1, 3, 0)]
 
     def project(to):
         at = pl.multiple_of(to * PIECE, PIECE)
@@ -665,8 +638,10 @@
         if PLANE[i] != (0, 0):
             back(i).wait_send()
     for chunk in range(2):
-        for k in range(9):
-            hop(chunk, k).wait_send()
+        for j in range(N_X):
+            along(chunk, j).wait_send()
+        for j in range(1, N_X):
+            forward(chunk, j).wait_send()
     for copy in sq_sends + ssq_sends:
         copy.wait_send()
     for k in range(N_X):
@@ -735,8 +710,8 @@
             pltpu.VMEM((N_VALUE, STEPS * STEPS * REPLACED, PIECE), BF16),
             pltpu.VMEM((N_VALUE, STEPS * STEPS * REPLACED, PIECE), BF16),
             dma((15,)),
-            dma((2, 9)),
-            dma((2, 9)),
+            dma((2, 2 * N_X - 1)),
+            dma((2, 2 * N_X - 1)),
             dma((N_X,)),
             dma((N_X,)),
             dma((N_X,)),

time: 44.1 us -> 39.4 us (0.89)
  Pallas kernels: 42.5 us -> 37.8 us
    pallas_call x1, Pallas kernels: 42.5 us -> 37.8 us  [on_device(): pl.pallas_call(kernel, out_shape=jax.ShapeDtypeStruct((STEPS * ROWS, PIEC...]
where the time goes in v4:
time: 39.4 us; the launch traced here: 39.3 us
  Pallas kernels  37.8 us (96%)
  local copies, waits for them, and re-layouts  1.47 us (4%)
    pallas_call x1, Pallas kernels, on_device(): pl.pallas_call(kernel, out_shape=jax.ShapeDtypeStruct((STEPS * ROWS, PIEC...  37.8 us
    unnamed x1, local copies, waits for them, and re-layouts  1.47 us

profile of v4, /device:TPU:1, one launch (start us, length us, event | category | flops | bytes accessed | tf_op | source)
XLA Modules:
  0.0 39.3 jit_solution(13675155308579010097)
XLA Ops:
  0.0 37.8 %delta_steps.1 = bf16[128,256]{1,0:T(8,128)(2,1)} custom-call(s32[4,2,16]{2,1,0:T(2,128)} %bitcast.7, s32[4,2,16]{2,1,0:T(2,128)} %bitcast.8, s32[4,2,16]{2,1,0:T(2,128)} %bitcast.9, f32[32]{0:T(128)} %logd_hbm.1, f32[32]{0:T(128)} %bias_hbm.1, f32[16]{0:T(128)} %gain_hbm.1, bf16[4,32,2048]{2,1,0:T(8,128)(2,1)} %x_hbm.1, bf16[2048,512]{1,0:T(8,128)(2,1)} %wqk_hbm.1, ...), custom_call_target="tpu_custom_call" | custom-call | tf_op jit(solution)/shard_map/delta_steps/pallas_call | solution.py:673
  37.8 1.5 %copy.16 = bf16[4,32,256]{2,1,0:T(8,128)(2,1)} copy(bf16[4,32,256]{2,1,0:T(8,128)(2,1)} %bitcast.6) | data formatting | bytes 131072

commit v5 on v4

--- a/solution.py
+++ b/solution.py
@@ -40,6 +40,8 @@
 FIRST, LAST = 0, 1
 BASE = (0, 16)
 CHUNK = 16
+SLOT_ROWS = STEPS * STEPS * REPLACED
+SUMMED = (STEPS * CHUNK, STEPS * CHUNK + SLOT_ROWS)
 UNROLL = 8
 
 
@@ -110,8 +112,6 @@
     part,
     r2_snd,
     r2_rcv,
-    s_snd,
-    s_rcv,
     loc,
     ag_s,
     ag_r,
@@ -129,8 +129,6 @@
     r2r,
     sqs,
     sqr,
-    ss,
-    sr,
 ):
     me_d = lax.axis_index("dp")
     me_v = lax.axis_index("value")
@@ -145,6 +143,23 @@
     def peer(i):
         dz, dy = PLANE[i]
         return ((me_d // N_X + dz) % N_X) * N_X + (me_d % N_X + dy) % N_X
+
+    def load(src, dst, k):
+        cp = pltpu.make_async_copy(src, dst, loc.at[k])
+        cp.start()
+        return cp
+
+    l_x = load(x_hbm, x_v, 0)
+    l_qk = load(wqk_hbm, wqk_v, 1)
+    scalars = (
+        (fin_hbm, fin_ref),
+        (own_hbm, own_ref),
+        (slot_hbm, slot_ref),
+        (logd_hbm, logd_ref),
+        (bias_hbm, bias_ref),
+        (gain_hbm, gain_ref),
+    )
+    l_scalars = [load(src, dst, 9 + k) for k, (src, dst) in enumerate(scalars)]
 
     barrier = pltpu.get_barrier_semaphore()
     greeted = 0
@@ -158,22 +173,6 @@
         pl.semaphore_signal(barrier, inc=1, device_id=to, device_id_type=MESH)
         greeted += 1
 
-    def load(src, dst, k):
-        cp = pltpu.make_async_copy(src, dst, loc.at[k])
-        cp.start()
-        return cp
-
-    l_x = load(x_hbm, x_v, 0)
-    l_qk = load(wqk_hbm, wqk_v, 1)
-    scalars = (
-        (fin_hbm, fin_ref),
-        (own_hbm, own_ref),
-        (slot_hbm, slot_ref),
-        (logd_hbm, logd_ref),
-        (bias_hbm, bias_ref),
-        (gain_hbm, gain_ref),
-    )
-    l_scalars = [load(src, dst, 9 + k) for k, (src, dst) in enumerate(scalars)]
     l_r = load(wr_hbm, wr_v, 2)
     l_v = load(wv_hbm, wv_v, 3)
     l_g = load(wg_hbm, wg_v, 4)
@@ -181,11 +180,6 @@
     l_s = load(st_hbm, st_v, 6)
     l_o = load(wo_hbm, wo_v, 8)
 
-    l_x.wait()
-    l_qk.wait()
-    xin = x_v[...].reshape(STEPS * ROWS, WIDTH)
-    joined = dot(xin, wqk_v[...]).astype(BF16)
-    joined_f = joined.astype(F32)
     for copy in l_scalars:
         copy.wait()
     pick = jnp.zeros((N_DP, ROWS), F32)
@@ -194,6 +188,12 @@
             hit = (iota((N_DP, ROWS), 0) == own_ref[t, j, me_d]) & (iota((N_DP, ROWS), 1) == fin_ref[t, j, me_d])
             pick = jnp.where(hit, 1.0, pick)
     pick = pick.astype(BF16)
+
+    l_x.wait()
+    l_qk.wait()
+    xin = x_v[...].reshape(STEPS * ROWS, WIDTH)
+    joined = dot(xin, wqk_v[...]).astype(BF16)
+    joined_f = joined.astype(F32)
     for t in range(STEPS):
         chosen = dot(pick, joined[t * ROWS : (t + 1) * ROWS])
         for h in range(HEADS):
@@ -327,10 +327,16 @@
     gating = dot(xin, wg_v[...])
     for g in range(GROUPS):
         rowq[GATING + g * ALL : GATING + (g + 1) * ALL] = gating[:, g * 128 : (g + 1) * 128]
+    chosen_slots = []
+    for d in range(N_DP):
+        slot = jnp.int32(0)
+        for t in range(STEPS):
+            for j in range(REPLACED):
+                slot = jnp.where(own_ref[t, j, d] == me_d, slot_ref[t, j, d], slot)
+        chosen_slots.append(slot)
     for j in (0, 1, 3, 2):
         foreign_all(j).wait_recv()
         foreign_forward(j).start()
-    pass_on(FIRST)
 
     lane = iota((8, 128), 1)
     sub = iota((8, 128), 0)
@@ -367,21 +373,10 @@
         lax.fori_loop(0, count // UNROLL, some, 0)
 
     def foreign_rows():
-        def one(d):
-            slot = jnp.int32(0)
-            for t in range(STEPS):
-                for j in range(REPLACED):
-                    slot = jnp.where(own_ref[t, j, d] == me_d, slot_ref[t, j, d], slot)
+        for d in range(N_DP):
             qk = gbuf[:, ROWS + d].reshape(N_VALUE * TILE, DK)
-            blocks = contract(qk, pf_v[slot])
+            blocks = contract(qk, pf_v[chosen_slots[d]])
             rsnd[d] = jnp.concatenate(blocks, axis=0).astype(BF16)
-
-        def some(i, _):
-            for k in range(UNROLL):
-                one(UNROLL * i + k)
-            return 0
-
-        lax.fori_loop(0, N_DP // UNROLL, some, 0)
 
     def back(i):
         dst = peer(i)
@@ -402,36 +397,49 @@
         if PLANE[i] != (0, 0):
             back(i).start()
     rrcv[me_d] = rsnd[me_d]
-    pass_on(LAST)
-    l_s.wait()
-    all_here(FIRST)
-    own_rows(0, CHUNK)
-    all_here(LAST)
-    own_rows(CHUNK, CHUNK)
-
-    gram = [msc[GROUPS, pl.ds(k, ROWS, stride=8), :] for k in range(2 * STEPS)]
+
+    def row_get(chunk):
+        def get(at):
+            return rowq[at + BASE[chunk] : at + BASE[chunk] + CHUNK]
+
+        return get
+
     src = iota((DK, 128), 0)
     head = (iota((DK, 128), 1) % H) // 2
-    spread = [(src == 64 + head * 4 + s).astype(F32) for s in range(STEPS)]
-    exact = dict(precision=lax.Precision.HIGHEST)
-    by_key = dot(jnp.concatenate(gram, axis=0), jnp.concatenate(spread, axis=1), **exact)
-    inv_k, inv_q = [], []
-    for t in range(STEPS):
-        kk = by_key[(STEPS + t) * ROWS : (STEPS + t + 1) * ROWS, t * 128 : (t + 1) * 128]
-        qq = dot(gram[t], (src == head * 4 + t).astype(F32), **exact)
-        inv_k.append(lax.rsqrt(kk + 1e-06))
-        inv_q.append(lax.rsqrt(qq + 1e-06) * DK ** (-0.5))
-        rowq[INV_K + t * ROWS : INV_K + (t + 1) * ROWS] = inv_k[t]
-        rowq[INV_Q + t * ROWS : INV_Q + (t + 1) * ROWS] = inv_q[t]
-    for t in range(STEPS):
-        for s in range(t + 1):
+    spread = [src == 64 + head * 4 + s for s in range(STEPS)] + [src == head * 4 + t for t in range(STEPS)]
+    spread = jnp.concatenate([entry.astype(F32) for entry in spread], axis=1).astype(BF16)
+
+    def contractions(chunk):
+        def part_of(g, k):
+            return msc[g, pl.ds(BASE[chunk] * 8 + k, CHUNK, stride=8), :]
+
+        all_here(chunk)
+        own_rows(BASE[chunk], CHUNK)
+        gram = [part_of(GROUPS, k) for k in range(2 * STEPS)]
+        gram = jnp.concatenate(gram, axis=0)
+        high = gram.astype(BF16)
+        low = (gram - high.astype(F32)).astype(BF16)
+        copied = dot(jnp.concatenate([high, low], axis=0), spread)
+        copied = copied[: 2 * STEPS * CHUNK] + copied[2 * STEPS * CHUNK :]
+
+        def entry(k, s):
+            return copied[k * CHUNK : (k + 1) * CHUNK, s * 128 : (s + 1) * 128]
+
+        def put(at, what):
+            rowq[at + BASE[chunk] : at + BASE[chunk] + CHUNK] = what
+
+        inv_k, inv_q = [], []
+        for t in range(STEPS):
+            inv_k.append(lax.rsqrt(entry(STEPS + t, t) + 1e-06))
+            inv_q.append(lax.rsqrt(entry(t, STEPS + t) + 1e-06) * DK ** (-0.5))
+            put(INV_K + t * ROWS, inv_k[t])
+            put(INV_Q + t * ROWS, inv_q[t])
+        for s, t in PAIRS:
+            at = PAIRS.index((s, t)) * ROWS
             if s < t:
-                at = KEY_KEY + PAIRS.index((s, t)) * ROWS
-                kk = by_key[(STEPS + t) * ROWS : (STEPS + t + 1) * ROWS, s * 128 : (s + 1) * 128]
-                rowq[at : at + ROWS] = kk * (inv_k[s] * inv_k[t])
-            at = KEY_QUERY + PAIRS.index((s, t)) * ROWS
-            kq = by_key[t * ROWS : (t + 1) * ROWS, s * 128 : (s + 1) * 128]
-            rowq[at : at + ROWS] = kq * (inv_k[s] * inv_q[t])
+                put(KEY_KEY + at, entry(STEPS + t, s) * (inv_k[s] * inv_k[t]))
+            put(KEY_QUERY + at, entry(t, s) * (inv_k[s] * inv_q[t]))
+        return part_of
 
     def recurrence(get, contracted, fresh):
         readouts = [[None] * GROUPS for _ in range(STEPS)]
@@ -483,13 +491,13 @@
             out.append(lax.rsqrt(total * (1.0 / DV) + 1e-06))
         return out
 
-    def exchange(buf, s_sem, r_sem):
+    def exchange(place, s_sem, r_sem):
         def one(i, slot):
             return pltpu.make_async_remote_copy(
-                src_ref=buf.at[slot],
-                dst_ref=buf.at[slot],
-                send_sem=s_sem.at[i],
-                recv_sem=r_sem.at[i],
+                src_ref=place(slot),
+                dst_ref=place(slot),
+                send_sem=s_sem(i),
+                recv_sem=r_sem(i),
                 device_id=(me_d, (me_v + i) % N_VALUE),
                 device_id_type=MESH,
             )
@@ -498,15 +506,83 @@
         arrivals = [one(i, (me_v + N_VALUE - i) % N_VALUE) for i in range(1, N_VALUE)]
         return sends, arrivals
 
-    def row_get(at):
-        return rowq[at : at + ROWS]
-
-    readouts, packed = recurrence(row_get, lambda g, k: msc[g, pl.ds(k, ROWS, stride=8), :], None)
-    sqbuf[me_v] = packed.astype(BF16)
-    sq_sends, sq_arrivals = exchange(sqbuf, qs, qr)
-    for copy in sq_sends:
-        copy.start()
-
+    def first_half(chunk):
+        part_of = contractions(chunk)
+        readouts, packed = recurrence(row_get(chunk), part_of, None)
+        sqbuf[chunk, me_v] = packed.astype(BF16)
+        sends, arrivals = exchange(
+            lambda slot: sqbuf.at[chunk, slot], lambda i: qs.at[chunk, i], lambda i: qr.at[chunk, i]
+        )
+        for copy in sends:
+            copy.start()
+        return readouts, sends, arrivals
+
+    def scaled(chunk, readouts, arrivals):
+        for copy in arrivals:
+            copy.wait_recv()
+        scales = scalings(jnp.sum(sqbuf[chunk].astype(F32), axis=0))
+        for t in range(STEPS):
+            for g in range(GROUPS):
+                rows = slice(t * CHUNK, (t + 1) * CHUNK)
+                gat_s[chunk, rows, g * 128 : (g + 1) * 128] = (readouts[t][g] * scales[t]).astype(BF16)
+
+    order = [(x + j) % N_X for j in (2, 1, 3, 0)]
+
+    def project(what, to):
+        at = pl.multiple_of(to * PIECE, PIECE)
+        return dot(what, wo_v[:, pl.ds(at, PIECE)])
+
+    def first_copy(chunk, k):
+        return pltpu.make_async_remote_copy(
+            src_ref=r1_snd.at[chunk, k, pl.ds(0, SUMMED[chunk])],
+            dst_ref=r1_rcv.at[chunk, k, pl.ds(0, SUMMED[chunk])],
+            send_sem=r1s.at[chunk, k],
+            recv_sem=r1r.at[chunk, k],
+            device_id=(me_d, partner),
+            device_id_type=MESH,
+        )
+
+    def second_copy(chunk, k):
+        return pltpu.make_async_remote_copy(
+            src_ref=r2_snd.at[chunk, k, pl.ds(0, SUMMED[chunk])],
+            dst_ref=r2_rcv.at[chunk, k, pl.ds(0, SUMMED[chunk])],
+            send_sem=r2s.at[chunk, k],
+            recv_sem=r2r.at[chunk, k],
+            device_id=(me_d, vid(order[k], c)),
+            device_id_type=MESH,
+        )
+
+    def sum_over_cores(chunk):
+        n = SUMMED[chunk]
+        gated = gat_s[chunk, :n]
+        for k in range(N_X):
+            r1_snd[chunk, k, :n] = project(gated, vid(order[k], 1 - c)).astype(BF16)
+            first_copy(chunk, k).start()
+        for k in range(N_X):
+            part[chunk, k, :n] = project(gated, vid(order[k], c))
+
+    def sum_along_x(chunk):
+        n = SUMMED[chunk]
+        for k in range(N_X - 1):
+            first_copy(chunk, k).wait_recv()
+            r2_snd[chunk, k, :n] = (part[chunk, k, :n] + r1_rcv[chunk, k, :n].astype(F32)).astype(BF16)
+            second_copy(chunk, k).start()
+
+    def summed(chunk):
+        n = SUMMED[chunk]
+        first_copy(chunk, 3).wait_recv()
+        total = part[chunk, 3, :n] + r1_rcv[chunk, 3, :n].astype(F32)
+        for k in (1, 2, 0):
+            second_copy(chunk, k).wait_recv()
+            total = total + r2_rcv[chunk, k, :n].astype(F32)
+        return total
+
+    l_s.wait()
+    pass_on(FIRST)
+    pass_on(LAST)
+    readouts_a, sq_sends_a, sq_arrivals_a = first_half(FIRST)
+    silu_gain(readouts_a, row_get(FIRST))
+    readouts_b, sq_sends_b, sq_arrivals_b = first_half(LAST)
     slots = [(t, j) for t in range(STEPS) for j in range(REPLACED)]
     for k, (t, j) in enumerate(slots):
         slotq[k * QUANTITIES : (k + 1) * QUANTITIES] = rowq[pl.ds(fin_ref[t, j, me_d], QUANTITIES, stride=ROWS), :]
@@ -514,7 +590,6 @@
     def slot_get(at):
         return slotq[pl.ds(at // ROWS, len(slots), stride=QUANTITIES), :]
 
-    silu_gain(readouts, row_get)
     slot_of = jnp.full((ALL, 128), -1, jnp.int32)
     take_of = jnp.full((ALL, len(slots) * STEPS), -1, jnp.int32)
     for k, (t, j) in enumerate(slots):
@@ -538,60 +613,21 @@
         [slot_row // REPLACED == t for t in range(STEPS)],
     )
     ssqbuf[me_v] = slot_packed
-    ssq_sends, ssq_arrivals = exchange(ssqbuf, sqs, sqr)
+    ssq_sends, ssq_arrivals = exchange(lambda slot: ssqbuf.at[slot], lambda i: sqs.at[i], lambda i: sqr.at[i])
     for copy in ssq_sends:
         copy.start()
+    l_o.wait()
+    scaled(FIRST, readouts_a, sq_arrivals_a)
+    sum_over_cores(FIRST)
+    silu_gain(readouts_b, row_get(LAST))
     silu_gain(slot_readouts, slot_get)
-
-    for copy in sq_arrivals:
-        copy.wait_recv()
-    scales = scalings(jnp.sum(sqbuf[...].astype(F32), axis=0))
-    for t in range(STEPS):
-        for g in range(GROUPS):
-            gat_s[t * ROWS : (t + 1) * ROWS, g * 128 : (g + 1) * 128] = (readouts[t][g] * scales[t]).astype(BF16)
-
-    l_o.wait()
-    gated = gat_s[...]
-    order = [(x + j) % N_X for j in (2, 1, 3, 0)]
-
-    def project(to):
-        at = pl.multiple_of(to * PIECE, PIECE)
-        return dot(gated, wo_v[:, pl.ds(at, PIECE)])
-
-    def first_copy(k):
-        return pltpu.make_async_remote_copy(
-            src_ref=r1_snd.at[k],
-            dst_ref=r1_rcv.at[k],
-            send_sem=r1s.at[k],
-            recv_sem=r1r.at[k],
-            device_id=(me_d, partner),
-            device_id_type=MESH,
-        )
-
-    def second_copy(k):
-        return pltpu.make_async_remote_copy(
-            src_ref=r2_snd.at[k],
-            dst_ref=r2_rcv.at[k],
-            send_sem=r2s.at[k],
-            recv_sem=r2r.at[k],
-            device_id=(me_d, vid(order[k], c)),
-            device_id_type=MESH,
-        )
-
-    for k in range(N_X):
-        r1_snd[k] = project(vid(order[k], 1 - c)).astype(BF16)
-        first_copy(k).start()
-    for k in range(N_X):
-        part[k] = project(vid(order[k], c))
-    for k in range(N_X - 1):
-        first_copy(k).wait_recv()
-        r2_snd[k] = (part[k] + r1_rcv[k].astype(F32)).astype(BF16)
-        second_copy(k).start()
+    sum_along_x(FIRST)
+    scaled(LAST, readouts_b, sq_arrivals_b)
 
     for copy in ssq_arrivals:
         copy.wait_recv()
     slot_scales = scalings(jnp.sum(ssqbuf[...], axis=0))
-    slot_gated = jnp.concatenate(
+    gat_s[LAST, SUMMED[FIRST] : SUMMED[LAST]] = jnp.concatenate(
         [
             jnp.concatenate([slot_readouts[t][g] * slot_scales[t] for g in range(GROUPS)], axis=1)
             for t in range(STEPS)
@@ -599,37 +635,18 @@
         axis=0,
     ).astype(BF16)
 
-    def slot_project(to):
-        at = pl.multiple_of(to * PIECE, PIECE)
-        return dot(slot_gated, wo_v[:, pl.ds(at, PIECE)])
-
-    def slot_copy(i):
-        return pltpu.make_async_remote_copy(
-            src_ref=s_snd.at[i],
-            dst_ref=s_rcv.at[i],
-            send_sem=ss.at[i],
-            recv_sem=sr.at[i],
-            device_id=(me_d, (me_v + i) % N_VALUE),
-            device_id_type=MESH,
-        )
-
-    for i in (4, 3, 5, 2, 6, 1, 7):
-        s_snd[i] = slot_project((me_v + i) % N_VALUE).astype(BF16)
-        slot_copy(i).start()
-    slot_total = slot_project(me_v)
-
-    first_copy(3).wait_recv()
-    total = part[3] + r1_rcv[3].astype(F32)
-    for k in (1, 2, 0):
-        second_copy(k).wait_recv()
-        total = total + r2_rcv[k].astype(F32)
-    for i in (1, 7, 2, 6, 3, 5, 4):
-        slot_copy(i).wait_recv()
-        slot_total = slot_total + s_rcv[i].astype(F32)
-    chosen = dot(take, slot_total.astype(BF16))
+    sum_over_cores(LAST)
+    sum_along_x(LAST)
+
+    totals = [summed(FIRST), summed(LAST)]
+    chosen = dot(take, totals[LAST][SUMMED[FIRST] :].astype(BF16))
     for half in range(PIECE // 128):
         lanes = slice(half * 128, (half + 1) * 128)
-        out_ref[:, lanes] = jnp.where(slot_of >= 0, chosen[:, lanes], total[:, lanes]).astype(BF16)
+        for chunk, total in enumerate(totals):
+            for t in range(STEPS):
+                rows = slice(t * ROWS + BASE[chunk], t * ROWS + BASE[chunk] + CHUNK)
+                own = total[t * CHUNK : (t + 1) * CHUNK, lanes]
+                out_ref[rows, lanes] = jnp.where(slot_of[rows] >= 0, chosen[rows, lanes], own).astype(BF16)
 
     for j in range(N_X):
         foreign_all(j).wait_send()
@@ -642,14 +659,12 @@
             along(chunk, j).wait_send()
         for j in range(1, N_X):
             forward(chunk, j).wait_send()
-    for copy in sq_sends + ssq_sends:
+        for k in range(N_X):
+            first_copy(chunk, k).wait_send()
+        for k in range(N_X - 1):
+            second_copy(chunk, k).wait_send()
+    for copy in sq_sends_a + sq_sends_b + ssq_sends:
         copy.wait_send()
-    for k in range(N_X):
-        first_copy(k).wait_send()
-    for k in range(N_X - 1):
-        second_copy(k).wait_send()
-    for i in range(1, N_VALUE):
-        slot_copy(i).wait_send()
 
 
 def on_device(
@@ -699,16 +714,14 @@
             pltpu.VMEM((STEPS * REPLACED * GROUPS * 8, 128), F32),
             pltpu.VMEM((QUANTITIES * ROWS, 128), F32),
             pltpu.VMEM((STEPS * REPLACED * QUANTITIES, 128), F32),
-            pltpu.VMEM((STEPS * ROWS, COLS), BF16),
-            pltpu.VMEM((N_VALUE, ROWS, 128), BF16),
+            pltpu.VMEM((2, SUMMED[LAST], COLS), BF16),
+            pltpu.VMEM((2, N_VALUE, CHUNK, 128), BF16),
             pltpu.VMEM((N_VALUE, STEPS * REPLACED, 128), F32),
-            pltpu.VMEM((N_X, STEPS * ROWS, PIECE), BF16),
-            pltpu.VMEM((N_X, STEPS * ROWS, PIECE), BF16),
-            pltpu.VMEM((N_X, STEPS * ROWS, PIECE), F32),
-            pltpu.VMEM((N_X - 1, STEPS * ROWS, PIECE), BF16),
-            pltpu.VMEM((N_X - 1, STEPS * ROWS, PIECE), BF16),
-            pltpu.VMEM((N_VALUE, STEPS * STEPS * REPLACED, PIECE), BF16),
-            pltpu.VMEM((N_VALUE, STEPS * STEPS * REPLACED, PIECE), BF16),
+            pltpu.VMEM((2, N_X, SUMMED[LAST], PIECE), BF16),
+            pltpu.VMEM((2, N_X, SUMMED[LAST], PIECE), BF16),
+            pltpu.VMEM((2, N_X, SUMMED[LAST], PIECE), F32),
+            pltpu.VMEM((2, N_X - 1, SUMMED[LAST], PIECE), BF16),
+            pltpu.VMEM((2, N_X - 1, SUMMED[LAST], PIECE), BF16),
             dma((15,)),
             dma((2, 2 * N_X - 1)),
             dma((2, 2 * N_X - 1)),
@@ -718,14 +731,12 @@
             dma((N_X,)),
             dma((N_DP,)),
             dma((N_DP,)),
-            dma((N_VALUE,)),
-            dma((N_VALUE,)),
-            dma((N_X,)),
-            dma((N_X,)),
-            dma((N_X - 1,)),
-            dma((N_X - 1,)),
-            dma((N_VALUE,)),
-            dma((N_VALUE,)),
+            dma((2, N_VALUE)),
+            dma((2, N_VALUE)),
+            dma((2, N_X)),
+            dma((2, N_X)),
+            dma((2, N_X - 1)),
+            dma((2, N_X - 1)),
             dma((N_VALUE,)),
             dma((N_VALUE,)),
         ],

time: 39.4 us -> 38 us (0.964)
  Pallas kernels: 37.8 us -> 36.4 us
    pallas_call x1, Pallas kernels: 37.8 us -> 36.4 us  [on_device(): pl.pallas_call(kernel, out_shape=jax.ShapeDtypeStruct((STEPS * ROWS, PIEC...]
where the time goes in v5:
time: 38 us; the launch traced here: 37.9 us
  Pallas kernels  36.4 us (96%)
  local copies, waits for them, and re-layouts  1.47 us (4%)
    pallas_call x1, Pallas kernels, on_device(): pl.pallas_call(kernel, out_shape=jax.ShapeDtypeStruct((STEPS * ROWS, PIEC...  36.4 us
    unnamed x1, local copies, waits for them, and re-layouts  1.47 us

profile of v5, /device:TPU:1, one launch (start us, length us, event | category | flops | bytes accessed | tf_op | source)
XLA Modules:
  0.0 37.9 jit_solution(495031129842236583)
XLA Ops:
  0.0 36.4 %delta_steps.1 = bf16[128,256]{1,0:T(8,128)(2,1)} custom-call(s32[4,2,16]{2,1,0:T(2,128)} %bitcast.7, s32[4,2,16]{2,1,0:T(2,128)} %bitcast.8, s32[4,2,16]{2,1,0:T(2,128)} %bitcast.9, f32[32]{0:T(128)} %logd_hbm.1, f32[32]{0:T(128)} %bias_hbm.1, f32[16]{0:T(128)} %gain_hbm.1, bf16[4,32,2048]{2,1,0:T(8,128)(2,1)} %x_hbm.1, bf16[2048,512]{1,0:T(8,128)(2,1)} %wqk_hbm.1, ...), custom_call_target="tpu_custom_call" | custom-call | tf_op jit(solution)/shard_map/delta_steps/pallas_call | solution.py:688
  36.4 1.5 %copy.16 = bf16[4,32,256]{2,1,0:T(8,128)(2,1)} copy(bf16[4,32,256]{2,1,0:T(8,128)(2,1)} %bitcast.6) | data formatting | bytes 131072

commit v6 on v5

--- a/solution.py
+++ b/solution.py
@@ -42,7 +42,8 @@
 CHUNK = 16
 SLOT_ROWS = STEPS * STEPS * REPLACED
 SUMMED = (STEPS * CHUNK, STEPS * CHUNK + SLOT_ROWS)
-UNROLL = 8
+QK_PIECES = 4
+UNROLL = 16
 
 
 def ring(k):
@@ -149,8 +150,6 @@
         cp.start()
         return cp
 
-    l_x = load(x_hbm, x_v, 0)
-    l_qk = load(wqk_hbm, wqk_v, 1)
     scalars = (
         (fin_hbm, fin_ref),
         (own_hbm, own_ref),
@@ -160,6 +159,9 @@
         (gain_hbm, gain_ref),
     )
     l_scalars = [load(src, dst, 9 + k) for k, (src, dst) in enumerate(scalars)]
+    l_x = load(x_hbm, x_v, 0)
+    pieces = [pl.ds(k * (WIDTH // QK_PIECES), WIDTH // QK_PIECES) for k in range(QK_PIECES)]
+    l_qk = [load(wqk_hbm.at[piece], wqk_v.at[piece], 15 + k) for k, piece in enumerate(pieces)]
 
     barrier = pltpu.get_barrier_semaphore()
     greeted = 0
@@ -190,9 +192,13 @@
     pick = pick.astype(BF16)
 
     l_x.wait()
-    l_qk.wait()
     xin = x_v[...].reshape(STEPS * ROWS, WIDTH)
-    joined = dot(xin, wqk_v[...]).astype(BF16)
+    joined = jnp.zeros((ALL, COLS), F32)
+    for k, piece in enumerate(pieces):
+        l_qk[k].wait()
+        deep = slice(k * (WIDTH // QK_PIECES), (k + 1) * (WIDTH // QK_PIECES))
+        joined = joined + dot(xin[:, deep], wqk_v[piece])
+    joined = joined.astype(BF16)
     joined_f = joined.astype(F32)
     for t in range(STEPS):
         chosen = dot(pick, joined[t * ROWS : (t + 1) * ROWS])
@@ -370,7 +376,10 @@
                 one(first + UNROLL * i + k)
             return 0
 
-        lax.fori_loop(0, count // UNROLL, some, 0)
+        if count == UNROLL:
+            some(0, 0)
+        else:
+            lax.fori_loop(0, count // UNROLL, some, 0)
 
     def foreign_rows():
         for d in range(N_DP):
@@ -506,8 +515,7 @@
         arrivals = [one(i, (me_v + N_VALUE - i) % N_VALUE) for i in range(1, N_VALUE)]
         return sends, arrivals
 
-    def first_half(chunk):
-        part_of = contractions(chunk)
+    def first_half(chunk, part_of):
         readouts, packed = recurrence(row_get(chunk), part_of, None)
         sqbuf[chunk, me_v] = packed.astype(BF16)
         sends, arrivals = exchange(
@@ -580,9 +588,8 @@
     l_s.wait()
     pass_on(FIRST)
     pass_on(LAST)
-    readouts_a, sq_sends_a, sq_arrivals_a = first_half(FIRST)
-    silu_gain(readouts_a, row_get(FIRST))
-    readouts_b, sq_sends_b, sq_arrivals_b = first_half(LAST)
+    readouts_a, sq_sends_a, sq_arrivals_a = first_half(FIRST, contractions(FIRST))
+    part_of_b = contractions(LAST)
     slots = [(t, j) for t in range(STEPS) for j in range(REPLACED)]
     for k, (t, j) in enumerate(slots):
         slotq[k * QUANTITIES : (k + 1) * QUANTITIES] = rowq[pl.ds(fin_ref[t, j, me_d], QUANTITIES, stride=ROWS), :]
@@ -616,6 +623,8 @@
     ssq_sends, ssq_arrivals = exchange(lambda slot: ssqbuf.at[slot], lambda i: sqs.at[i], lambda i: sqr.at[i])
     for copy in ssq_sends:
         copy.start()
+    readouts_b, sq_sends_b, sq_arrivals_b = first_half(LAST, part_of_b)
+    silu_gain(readouts_a, row_get(FIRST))
     l_o.wait()
     scaled(FIRST, readouts_a, sq_arrivals_a)
     sum_over_cores(FIRST)
@@ -687,7 +696,7 @@
     dma = pltpu.SemaphoreType.DMA
     produced = pl.pallas_call(
         kernel,
-        out_shape=jax.ShapeDtypeStruct((STEPS * ROWS, PIECE), BF16),
+        out_shape=pltpu.VMEM((STEPS * ROWS, PIECE), BF16),
         in_specs=[hbm] * 14,
         out_specs=pl.BlockSpec(memory_space=pltpu.VMEM),
         scratch_shapes=[
@@ -722,7 +731,7 @@
             pltpu.VMEM((2, N_X, SUMMED[LAST], PIECE), F32),
             pltpu.VMEM((2, N_X - 1, SUMMED[LAST], PIECE), BF16),
             pltpu.VMEM((2, N_X - 1, SUMMED[LAST], PIECE), BF16),
-            dma((15,)),
+            dma((15 + QK_PIECES,)),
             dma((2, 2 * N_X - 1)),
             dma((2, 2 * N_X - 1)),
             dma((N_X,)),

time: 38 us -> 36.4 us (0.958)
  local copies, waits for them, and re-layouts: 1.47 us -> 0.63 us
  Pallas kernels: 36.4 us -> 35.7 us
    unnamed x1, local copies, waits for them, and re-layouts: 1.47 us -> 0.63 us
    pallas_call x1, Pallas kernels: 36.4 us -> 35.7 us  [on_device(): pl.pallas_call(kernel, out_shape=pltpu.VMEM((STEPS * ROWS, PIECE), BF16),...]
where the time goes in v6:
time: 36.4 us; the launch traced here: 36.3 us
  Pallas kernels  35.7 us (98%)
  local copies, waits for them, and re-layouts  0.63 us (2%)
    pallas_call x1, Pallas kernels, on_device(): pl.pallas_call(kernel, out_shape=pltpu.VMEM((STEPS * ROWS, PIECE), BF16),...  35.7 us

profile of v6, /device:TPU:1, one launch (start us, length us, event | category | flops | bytes accessed | tf_op | source)
XLA Modules:
  0.0 36.3 jit_solution(9649643546533906767)
XLA Ops:
  0.0 35.7 %delta_steps.1 = bf16[128,256]{1,0:T(8,128)(2,1)S(1)} custom-call(s32[4,2,16]{2,1,0:T(2,128)} %bitcast.7, s32[4,2,16]{2,1,0:T(2,128)} %bitcast.8, s32[4,2,16]{2,1,0:T(2,128)} %bitcast.9, f32[32]{0:T(128)} %logd_hbm.1, f32[32]{0:T(128)} %bias_hbm.1, f32[16]{0:T(128)} %gain_hbm.1, bf16[4,32,2048]{2,1,0:T(8,128)(2,1)} %x_hbm.1, bf16[2048,512]{1,0:T(8,128)(2,1)} %wqk_hbm.1, ...), custom_call_target="tpu_custom_call" | custom-call | tf_op jit(solution)/shard_map/delta_steps/pallas_call | solution.py:697
  35.7 0.6 %copy.16 = bf16[4,32,256]{2,1,0:T(8,128)(2,1)} copy(bf16[4,32,256]{2,1,0:T(8,128)(2,1)S(1)} %bitcast.5) | data formatting | bytes 131072

commit v7 on v6

--- a/solution.py
+++ b/solution.py
@@ -334,7 +334,8 @@
     for g in range(GROUPS):
         rowq[GATING + g * ALL : GATING + (g + 1) * ALL] = gating[:, g * 128 : (g + 1) * 128]
     chosen_slots = []
-    for d in range(N_DP):
+    for i in range(N_DP):
+        d = peer(i)
         slot = jnp.int32(0)
         for t in range(STEPS):
             for j in range(REPLACED):
@@ -381,10 +382,11 @@
         else:
             lax.fori_loop(0, count // UNROLL, some, 0)
 
-    def foreign_rows():
-        for d in range(N_DP):
+    def foreign_rows(first, end):
+        for i in range(first, end):
+            d = peer(i)
             qk = gbuf[:, ROWS + d].reshape(N_VALUE * TILE, DK)
-            blocks = contract(qk, pf_v[chosen_slots[d]])
+            blocks = contract(qk, pf_v[chosen_slots[i]])
             rsnd[d] = jnp.concatenate(blocks, axis=0).astype(BF16)
 
     def back(i):
@@ -401,10 +403,11 @@
     l_p.wait()
     for j in (0, 1, 3, 2):
         foreign_forwarded(j)
-    foreign_rows()
-    for i in range(N_DP):
-        if PLANE[i] != (0, 0):
-            back(i).start()
+    for first in range(0, N_DP, N_DP // 2):
+        foreign_rows(first, first + N_DP // 2)
+        for i in range(first, first + N_DP // 2):
+            if PLANE[i] != (0, 0):
+                back(i).start()
     rrcv[me_d] = rsnd[me_d]
 
     def row_get(chunk):
@@ -576,6 +579,12 @@
             r2_snd[chunk, k, :n] = (part[chunk, k, :n] + r1_rcv[chunk, k, :n].astype(F32)).astype(BF16)
             second_copy(chunk, k).start()
 
+    def sums_left(chunk):
+        for k in range(N_X):
+            first_copy(chunk, k).wait_send()
+        for k in range(N_X - 1):
+            second_copy(chunk, k).wait_send()
+
     def summed(chunk):
         n = SUMMED[chunk]
         first_copy(chunk, 3).wait_recv()
@@ -631,6 +640,19 @@
     silu_gain(readouts_b, row_get(LAST))
     silu_gain(slot_readouts, slot_get)
     sum_along_x(FIRST)
+    for j in range(N_X):
+        foreign_all(j).wait_send()
+        foreign_forward(j).wait_send()
+    for i in range(N_DP):
+        if PLANE[i] != (0, 0):
+            back(i).wait_send()
+    for chunk in (FIRST, LAST):
+        for j in range(N_X):
+            along(chunk, j).wait_send()
+        for j in range(1, N_X):
+            forward(chunk, j).wait_send()
+    for copy in sq_sends_a:
+        copy.wait_send()
     scaled(LAST, readouts_b, sq_arrivals_b)
 
     for copy in ssq_arrivals:
@@ -647,7 +669,11 @@
     sum_over_cores(LAST)
     sum_along_x(LAST)
 
-    totals = [summed(FIRST), summed(LAST)]
+    for copy in sq_sends_b + ssq_sends:
+        copy.wait_send()
+    first_total = summed(FIRST)
+    sums_left(FIRST)
+    totals = [first_total, summed(LAST)]
     chosen = dot(take, totals[LAST][SUMMED[FIRST] :].astype(BF16))
     for half in range(PIECE // 128):
         lanes = slice(half * 128, (half + 1) * 128)
@@ -657,23 +683,7 @@
                 own = total[t * CHUNK : (t + 1) * CHUNK, lanes]
                 out_ref[rows, lanes] = jnp.where(slot_of[rows] >= 0, chosen[rows, lanes], own).astype(BF16)
 
-    for j in range(N_X):
-        foreign_all(j).wait_send()
-        foreign_forward(j).wait_send()
-    for i in range(N_DP):
-        if PLANE[i] != (0, 0):
-            back(i).wait_send()
-    for chunk in range(2):
-        for j in range(N_X):
-            along(chunk, j).wait_send()
-        for j in range(1, N_X):
-            forward(chunk, j).wait_send()
-        for k in range(N_X):
-            first_copy(chunk, k).wait_send()
-        for k in range(N_X - 1):
-            second_copy(chunk, k).wait_send()
-    for copy in sq_sends_a + sq_sends_b + ssq_sends:
-        copy.wait_send()
+    sums_left(LAST)
 
 
 def on_device(
@@ -714,15 +724,15 @@
             pltpu.VMEM((COLS, WIDTH), BF16),
             pltpu.VMEM((ROWS, 16, H, DK), F32),
             pltpu.VMEM((16, 16, H, DK), F32),
-            pltpu.VMEM((TILE * BLOCKS, DK), F32),
+            pltpu.VMEM(((TILE + 1) * BLOCKS, DK), F32),
             pltpu.VMEM((N_DP, TILE, DK), BF16),
             pltpu.VMEM((N_VALUE, BLOCKS, TILE, DK), BF16),
-            pltpu.VMEM((GROUPS + 1, ROWS * 8, 128), F32),
+            pltpu.VMEM((GROUPS + 1, (ROWS + 1) * 8, 128), F32),
             pltpu.VMEM((N_DP, GROUPS * 8, 128), BF16),
             pltpu.VMEM((N_DP, GROUPS * 8, 128), BF16),
-            pltpu.VMEM((STEPS * REPLACED * GROUPS * 8, 128), F32),
-            pltpu.VMEM((QUANTITIES * ROWS, 128), F32),
-            pltpu.VMEM((STEPS * REPLACED * QUANTITIES, 128), F32),
+            pltpu.VMEM(((STEPS * REPLACED + 1) * GROUPS * 8, 128), F32),
+            pltpu.VMEM(((QUANTITIES + 1) * ROWS, 128), F32),
+            pltpu.VMEM(((STEPS * REPLACED + 1) * QUANTITIES, 128), F32),
             pltpu.VMEM((2, SUMMED[LAST], COLS), BF16),
             pltpu.VMEM((2, N_VALUE, CHUNK, 128), BF16),
             pltpu.VMEM((N_VALUE, STEPS * REPLACED, 128), F32),

time: 36.4 us -> 36.3 us (level)
  no operation moved by 1% of the time
where the time goes in v7:
time: 36.3 us; the launch traced here: 36.2 us
  Pallas kernels  35.6 us (98%)
  local copies, waits for them, and re-layouts  0.63 us (2%)
    pallas_call x1, Pallas kernels, on_device(): pl.pallas_call(kernel, out_shape=pltpu.VMEM((STEPS * ROWS, PIECE), BF16),...  35.6 us

profile of v7, /device:TPU:1, one launch (start us, length us, event | category | flops | bytes accessed | tf_op | source)
XLA Modules:
  0.0 36.2 jit_solution(1297474718656807446)
XLA Ops:
  0.0 35.6 %delta_steps.1 = bf16[128,256]{1,0:T(8,128)(2,1)S(1)} custom-call(s32[4,2,16]{2,1,0:T(2,128)} %bitcast.7, s32[4,2,16]{2,1,0:T(2,128)} %bitcast.8, s32[4,2,16]{2,1,0:T(2,128)} %bitcast.9, f32[32]{0:T(128)} %logd_hbm.1, f32[32]{0:T(128)} %bias_hbm.1, f32[16]{0:T(128)} %gain_hbm.1, bf16[4,32,2048]{2,1,0:T(8,128)(2,1)} %x_hbm.1, bf16[2048,512]{1,0:T(8,128)(2,1)} %wqk_hbm.1, ...), custom_call_target="tpu_custom_call" | custom-call | tf_op jit(solution)/shard_map/delta_steps/pallas_call | solution.py:707
  35.6 0.6 %copy.16 = bf16[4,32,256]{2,1,0:T(8,128)(2,1)} copy(bf16[4,32,256]{2,1,0:T(8,128)(2,1)S(1)} %bitcast.5) | data formatting | bytes 131072
